TPU v7x, 128 devices: a whole 4x4x4 slice. The times are simulated.
128 devices in a mesh: grp: 2 (over y_lo), dom: 64 (over x, z, y_hi, core).
Axes of the slice: x: 4, y: 4 (y_hi: 2, y_lo: 2; y = y_hi * 2 + y_lo), z: 4, core: 2. Of those that a mesh axis runs over, the one named last changes fastest.
Arguments:
- atm_state: float32 [2, 16, 2048, 2048], P(None, None, ('grp', 'dom')), may hold values from -6 to 6
- ocean_state: float32 [2, 16, 512, 512], P(None, None, 'dom', 'grp'), may hold values from -6 to 6
- atm_levels: float32 [16, 16], replicated, may hold values from -1.5 to 1.5
- ocean_levels: float32 [16, 16], replicated, may hold values from -1.5 to 1.5
- tile_weight: bfloat16 [32768, 128, 128], P(('grp', 'dom')), may hold values from 0 to 0.049804688
- tile_owner: int32 [32768, 1], P(('grp', 'dom')), may hold values from 0 to 127; in each aligned block of 256 rows (0 to 255, 256 to 511, ...) at most 3 rows name the same one
- tile_block: int32 [32768], P(('grp', 'dom')), may hold values from 0 to 15
- tile_source: int32 [32768], P(('grp', 'dom')), may hold values from 0 to 255
- tile_count: int32 [128], P(('grp', 'dom')), may hold values from 128 to 256, as said below
Outputs:
- atm_final: float32 [2, 16, 2048, 2048], P(None, None, ('grp', 'dom'))
- ocean_final: float32 [2, 16, 512, 512], P(None, None, 'dom', 'grp')
Inputs may be any that keep to these rules, and one draw needn't show every extreme that they name: `tile_owner`: among the 256 entries of one device's list, at most 3 name the same ocean device, live or not. `tile_count`: entries of a device's list at or past its count are padding and are ignored; some device's count is 256.
All inputs are finite; a program needn't handle non-finite values.
Results may differ from a plain program's by a relative error of at most 0.002.
Values may be sent and summed in bfloat16 or wider, within the bound.
No kernel may reach another device: no remote copies, remote signals or barrier semaphores. Data moves between devices by JAX's collectives and lax.ppermute only.
A program may use at most 128 MiB of HBM per device.

v0:
```python
import functools
import math

import jax
import jax.numpy as jnp
from jax import lax
from jax.experimental import pallas as pl
from jax.experimental.pallas import tpu as pltpu
from jax.sharding import PartitionSpec as P

STEPS = 4
HALO = STEPS
CAP = 3
ROWS = 8
LANES = 128
GROUP = 8
PAD = 8
WIDE = 2048
RING = ("grp", "dom")
F32 = jnp.float32
BF16 = jnp.bfloat16

diffuse = 0.2
vertical = 0.25
couple = 0.5
MIB = 1 << 20


VMEM = pl.BlockSpec(memory_space=pltpu.VMEM)
HBM = pl.BlockSpec(memory_space=pltpu.HBM)
SMEM = pl.BlockSpec(memory_space=pltpu.SMEM)


def params(mib):
    return pltpu.CompilerParams(vmem_limit_bytes=mib * MIB)


def cost(flops, mib):
    return pl.CostEstimate(flops=flops, bytes_accessed=mib * MIB, transcendentals=0)


def fetch(pairs, sems):
    copies = []
    for n, (source, target) in enumerate(pairs):
        copies.append(pltpu.make_async_copy(source, target, sems.at[n]))
        copies[-1].start()
    return copies


def iota(shape, dim):
    return lax.broadcasted_iota(jnp.int32, shape, dim)


def onehot(mask):
    return jnp.where(mask, 1.0, 0.0).astype(BF16)


def split(value):
    high = value.astype(BF16)
    return high, (value - high.astype(F32)).astype(BF16)


def mxu(left, right, dims=((1,), (0,))):
    return lax.dot_general(left, right, (dims, ((), ())), preferred_element_type=F32)


def exact(left, right):
    return lax.dot_general(
        left, right, (((1,), (0,)), ((), ())), precision=lax.Precision.HIGHEST,
        preferred_element_type=F32,
    )


def column(row):
    n = row.shape[1]
    eye = iota((n, n), 0) == iota((n, n), 1)
    return jnp.sum(jnp.where(eye, jnp.broadcast_to(row, (n, n)), 0.0), axis=1, keepdims=True)


def select_rows(state, offset):
    rows = state.shape[0]
    deep = rows // 16
    out, col = iota((16 * HALO, rows), 0), iota((16 * HALO, rows), 1)
    return mxu(onehot(col == (out >> 2) * deep + (out & 3) + offset % deep), state)


def coefficients():
    table = []
    for s in range(STEPS):
        by_level = []
        for i in range(STEPS - s + 1):
            by_distance = [0.0] * (STEPS + 1)
            for k in range(s, STEPS - i + 1, 2):
                q = STEPS - k - i
                trinomial = [1]
                for _ in range(q):
                    padded = [0, 0] + trinomial + [0, 0]
                    trinomial = [sum(padded[j : j + 3]) for j in range(len(trinomial) + 2)]
                scale = math.comb(k, (k - s) // 2) * math.comb(STEPS, k)
                scale *= math.comb(STEPS - k, i) * diffuse ** (k + q)
                for d in range(q + 1):
                    by_distance[d] += scale * trinomial[q + d]
            by_level.append(by_distance)
        table.append(by_level)
    return table


def lookup(weights, distance):
    total = 0.0
    for d, weight in enumerate(weights):
        if weight:
            total = jnp.where(distance == d, weight, total)
    return total


def stencils(own, image):
    table = coefficients()
    x = iota((16, LANES), 1) & (own - 1)
    r = iota((16, LANES), 0)
    sources = [(r & (own - 1), own), ((r & 3) - HALO, HALO), ((r & 3) + own, HALO)]
    result = [[[] for _ in by_level] for by_level in table]
    for xs, depth in sources:
        distance = jnp.abs(xs - x)
        if image is not None:
            first, last = image
            below = jnp.where(first == 1, jnp.abs(xs + x + 2), STEPS + 1)
            above = jnp.where(last == 1, jnp.abs(2 * own - xs - x), STEPS + 1)
            inside = ((first == 0) | (xs >= 0)) & ((last == 0) | (xs < own))
        for s, by_level in enumerate(table):
            for i, weights in enumerate(by_level):
                part = lookup(weights, distance)
                if image is not None:
                    part = part - lookup(weights, below) - lookup(weights, above)
                    part = jnp.where(inside, part, 0.0)
                result[s][i] += [part] * depth
    return [[jnp.concatenate(parts, axis=0) for parts in by_level] for by_level in result]


def small_product(left, right):
    total = 0.0
    for k in range(16):
        total = total + left[:, k : k + 1] * right[k : k + 1, :]
    return total


def operators(levels, own, image):
    rows, cols = 16 * own + 32 * HALO, 16 * own
    shift = own.bit_length() - 1
    one = vertical * levels.T[:16]
    two = small_product(one, one)
    stack = [half for p in (one, two, small_product(two, one), small_product(two, two))
             for half in split(p)]
    stack = jnp.concatenate([half.astype(F32) for half in stack], axis=0).astype(BF16)
    spread = onehot(iota((LANES, cols), 0) == (iota((LANES, cols), 1) >> shift))
    wide = mxu(stack, spread).astype(BF16)
    r, c = iota((rows, LANES), 0), iota((rows, LANES), 1)
    level = jnp.where(r < cols, r >> shift, (r >> 2) & 15)
    mixed = [mxu(onehot(((c & 15) == level) & ((c >> 5) == i)), wide) for i in range(STEPS)]
    r, c = iota((rows, cols), 0), iota((rows, cols), 1)
    same = jnp.where(r < cols, r >> shift, (r >> 2) & 15) == (c >> shift)
    result = []
    for by_level in stencils(own, image):
        total = 0.0
        for i, part in enumerate(by_level):
            part = jnp.concatenate([part] * (cols // LANES), axis=1)
            total = total + (jnp.where(same, part, 0.0) if i == 0 else part * mixed[i - 1])
        result.append(total)
    return result


def write_operators(edge_ref, levels, own_ref, halo_ref, ocean_ref):
    for s, part in enumerate(operators(levels[0], 16, None)):
        high, low = split(part[:256])
        lanes = slice((s & 1) * 256, (s & 1) * 256 + 256)
        if s < 2:
            own_ref[0:256, lanes] = low
            own_ref[256:512, lanes] = high
        else:
            own_ref[512:768, lanes] = high
        halo_ref[:, s * 256 : (s + 1) * 256] = part[256:].astype(BF16)
    image = (edge_ref[1], edge_ref[2])
    for s, part in enumerate(operators(levels[1], 8, image)):
        lanes = slice(s * LANES, (s + 1) * LANES)
        high, low = split(part[:128])
        ocean_ref[0:128, lanes] = low
        ocean_ref[128:256, lanes] = high
        ocean_ref[256:384, lanes] = part[128:].astype(BF16)


OWN, FAR, SEA = (768, 512), (128, 1024), (384, 512)


def mirror_low(rows):
    r = iota(rows.shape, 0)
    total = jnp.zeros_like(rows)
    for j in range(3):
        total = jnp.where(r == 6 - j, -rows[j : j + 1], total)
    return total


def mirror_high(rows):
    r = iota(rows.shape, 0)
    total = jnp.zeros_like(rows)
    for j in range(3):
        total = jnp.where(r == 1 + j, -rows[7 - j : 8 - j], total)
    return total


def halo_rows(halo, v):
    half = 16 * HALO
    empty = jnp.zeros((half, halo.shape[1]), halo.dtype)
    blocks = []
    for side in range(2):
        part = halo[side * half : (side + 1) * half]
        blocks += [part, empty] if v == 0 else [empty, part]
    return jnp.concatenate(blocks, axis=0)


def atmos_steps(v, arrivals, x_ref, low_ref, high_ref, own_ref, halo_ref, out_ref, surface_ref,
                left, main, minor, w, held, sems):
    chunks = len(arrivals)
    size = WIDE // chunks
    main[0:512] = own_ref[0:512]
    main[512:768] = own_ref[256:512]
    main[768:1024] = halo_rows(halo_ref[:, 0:512], v)
    minor[0:256] = own_ref[512:768]
    minor[256:512] = halo_rows(halo_ref[:, 512:1024], v)
    copies = []
    for n in range(chunks + 1):
        if n < chunks:
            arrivals[n].wait()
            start = n * size
            for c in range(size // LANES):
                rows = slice(c * LANES, (c + 1) * LANES)
                at = start + c * LANES
                for h in range(2):
                    state = x_ref[h * LANES : (h + 1) * LANES, at : at + LANES].T
                    high, low = split(state)
                    lanes = slice(h * LANES, (h + 1) * LANES)
                    w[STEPS, PAD + at : PAD + at + LANES, lanes] = state * diffuse**STEPS
                    left[rows, h * LANES : (h + 1) * LANES] = high
                    left[rows, 256 + h * LANES : 256 + (h + 1) * LANES] = low
                    left[rows, 512 + h * LANES : 512 + (h + 1) * LANES] = high
            left[:, 768:896] = low_ref[start : start + size]
            left[:, 896:1024] = high_ref[start : start + size]
            rows = slice(PAD + start, PAD + start + size)
            for s in range(2):
                lanes = slice(s * 256, (s + 1) * 256)
                w[s, rows] = mxu(left[...], main[:, lanes])
                w[2 + s, rows] = mxu(left[:, 512:1024], minor[:, lanes])
        if n == 0:
            for s in range(1, STEPS + 1):
                w[s, 0:PAD] = mirror_low(w[s, PAD : 2 * PAD])
        if n == chunks - 1:
            for s in range(1, STEPS + 1):
                w[s, WIDE + PAD : WIDE + 2 * PAD] = mirror_high(w[s, WIDE : WIDE + PAD])
        if n > 0:
            start = (n - 1) * size
            for c in range(size // LANES):
                at = PAD + start + c * LANES
                for h in range(2):
                    lanes = slice(h * LANES, (h + 1) * LANES)
                    total = w[0, at : at + LANES, lanes]
                    for s in range(1, STEPS + 1):
                        total += w[s, at - s : at - s + LANES, lanes]
                        total += w[s, at + s : at + s + LANES, lanes]
                    held[lanes, at - PAD : at - PAD + LANES] = total.T
            cells = pl.ds(start, size)
            surface_ref[:, start : start + size] = held[0:16, start : start + size]
            copy = pltpu.make_async_copy(
                held.at[:, cells], out_ref.at[v, :, cells], sems.at[n - 1]
            )
            copy.start()
            copies.append(copy)
    return copies


def atmos_scratch(chunks):
    size = WIDE // chunks
    return [
        pltpu.VMEM((256, WIDE), F32),
        pltpu.SemaphoreType.DMA((chunks,)),
        pltpu.VMEM((size, 1024), BF16),
        pltpu.VMEM((1024, 512), BF16),
        pltpu.VMEM((512, 512), BF16),
        pltpu.VMEM((STEPS + 1, WIDE + 2 * PAD, 256), F32),
        pltpu.VMEM((256, WIDE), F32),
        pltpu.SemaphoreType.DMA((chunks,)),
    ]


def fetch_atmos(v, atm_ref, x_ref, sems):
    size = WIDE // sems.shape[0]
    cells = [pl.ds(n * size, size) for n in range(sems.shape[0])]
    return fetch([(atm_ref.at[v, :, c], x_ref.at[:, c]) for c in cells], sems)


def edge_kernel(edge_ref, ocean_ref, low_ref, high_ref, out_ref):
    first = edge_ref[0] == 0
    for v in range(2):
        before, after = ocean_ref[v, :, 0:LANES].T[:PAD], ocean_ref[v, :, LANES:].T[LANES - PAD :]
        out_ref[v * PAD : (v + 1) * PAD] = jnp.where(first, after, before)
    for n, ref in enumerate((low_ref, high_ref)):
        before, after = ref[WIDE : WIDE + 16], ref[WIDE + 240 : WIDE + 256]
        edge = jnp.where(first, after.astype(F32)[16 - PAD :], before.astype(F32)[:PAD])
        out_ref[(2 + n) * PAD : (3 + n) * PAD] = edge


def edge_rows(edge, ocean, low, high):
    return pl.pallas_call(
        edge_kernel,
        in_specs=[SMEM, VMEM, VMEM, VMEM],
        out_specs=VMEM,
        out_shape=jax.ShapeDtypeStruct((4 * PAD, LANES), F32),
        compiler_params=params(16),
        name="ocean_edge",
    )(edge, ocean, low, high)


def early_kernel(
    edge_ref, atm_levels_ref, ocean_levels_ref, atm_ref, low_ref, high_ref,
    out_ref, surface_ref, own_out, halo_out, sea_out,
    levels, own, halo, sea, few, *rest,
):
    x_ref, x_sems = rest[:2]
    arrivals = fetch_atmos(0, atm_ref, x_ref, x_sems)
    levels[...] = jnp.zeros_like(levels)
    levels[0, 0:16, 0:16] = atm_levels_ref[...]
    levels[1, 0:16, 0:16] = ocean_levels_ref[...]
    write_operators(edge_ref, (levels[0], levels[1]), own, halo, sea)
    keep = fetch([(own, own_out), (halo, halo_out), (sea, sea_out)], few)
    sent = atmos_steps(
        0, arrivals, x_ref, low_ref, high_ref, own, halo, out_ref, surface_ref, *rest[2:]
    )
    for copy in keep + sent:
        copy.wait()


def early(edge, atm_levels, ocean_levels, atm, low, high, chunks=4):
    return pl.pallas_call(
        early_kernel,
        in_specs=[SMEM, VMEM, VMEM, HBM, VMEM, VMEM],
        out_specs=[HBM, VMEM, HBM, HBM, HBM],
        out_shape=[
            pltpu.HBM(atm.shape, F32),
            jax.ShapeDtypeStruct((16, WIDE), F32),
            pltpu.HBM(OWN, BF16),
            pltpu.HBM(FAR, BF16),
            pltpu.HBM(SEA, BF16),
        ],
        scratch_shapes=[
            pltpu.VMEM((2, LANES, LANES), F32),
            pltpu.VMEM(OWN, BF16),
            pltpu.VMEM(FAR, BF16),
            pltpu.VMEM(SEA, BF16),
            pltpu.SemaphoreType.DMA((3,)),
        ]
        + atmos_scratch(chunks),
        compiler_params=params(40),
        cost_estimate=cost(3 * 512 * 1024 * WIDE, 6),
        name="atmosphere_0",
    )(edge, atm_levels, ocean_levels, atm, low, high)


def ocean_steps(first, ocean_ref, low_ref, high_ref, side_ref, g_ref, flux_ref, out_ref, w):
    wide = ocean_ref.shape[2]

    def extend(rows, side):
        empty = jnp.zeros_like(side)
        before, after = jnp.where(first, empty, side), jnp.where(first, side, empty)
        return jnp.concatenate([before, rows, after], axis=0)

    halos = []
    for n, ref in enumerate((low_ref, high_ref)):
        side = side_ref[(2 + n) * PAD : (3 + n) * PAD]
        halos.append(extend(ref[WIDE : WIDE + wide].astype(F32), side).astype(BF16))
    for v in range(2):
        own = jnp.concatenate([ocean_ref[v, :, :LANES].T, ocean_ref[v, :, LANES:].T], axis=0)
        state = extend(own, side_ref[v * PAD : (v + 1) * PAD])
        high, low = split(state)
        left = jnp.concatenate([high, low, high] + halos, axis=1)
        g = g_ref[...]
        right = jnp.concatenate([g[:256], g[128:256], halo_rows(g[256:], v)], axis=0)
        for s in range(STEPS):
            w[s] = mxu(left, right[:, s * LANES : (s + 1) * LANES])
        w[STEPS] = state * diffuse**STEPS
        end = wide + PAD
        for s in range(1, STEPS + 1):
            w[s, 0:PAD] = jnp.where(first, mirror_low(w[s, PAD : 2 * PAD]), w[s, 0:PAD])
            w[s, end : end + PAD] = jnp.where(
                first, w[s, end : end + PAD], mirror_high(w[s, end - PAD : end])
            )
        for c in range(wide // LANES):
            at = PAD + c * LANES
            total = w[0, at : at + LANES]
            for s in range(1, STEPS + 1):
                total += w[s, at - s : at - s + LANES]
                total += w[s, at + s : at + s + LANES]
            final = total.T
            lanes = slice(c * LANES, (c + 1) * LANES)
            out_ref[v, :, lanes] = final
            out_ref[v, 0:8, lanes] = final[0:8] + couple * flux_ref[v, :, lanes]


def late_kernel(
    edge_ref, atm_ref, ocean_ref, low_ref, high_ref, side_ref, flux_ref, own_ref, halo_ref,
    sea_ref, _, out_ref, surface_ref, ocean_out, state, sea, own, halo, sea_w, few, *rest,
):
    x_ref, x_sems = rest[:2]
    arrivals = fetch(
        [(ocean_ref, state), (sea_ref, sea), (own_ref, own), (halo_ref, halo)], few
    )
    x_arrivals = fetch_atmos(1, atm_ref, x_ref, x_sems)
    for copy in arrivals:
        copy.wait()
    ocean_steps(
        edge_ref[0] == 0, state, low_ref, high_ref, side_ref, sea, flux_ref, ocean_out, sea_w
    )
    sent = atmos_steps(
        1, x_arrivals, x_ref, low_ref, high_ref, own, halo, out_ref, surface_ref, *rest[2:]
    )
    for copy in sent:
        copy.wait()


def late(edge, atm, ocean, low, high, side, flux, own, halo, sea, half, chunks=4):
    return pl.pallas_call(
        late_kernel,
        in_specs=[SMEM, HBM, HBM, VMEM, VMEM, VMEM, VMEM] + [HBM] * 4,
        out_specs=[HBM, VMEM, VMEM],
        out_shape=[
            pltpu.HBM(atm.shape, F32),
            jax.ShapeDtypeStruct((16, WIDE), F32),
            jax.ShapeDtypeStruct(ocean.shape, F32),
        ],
        scratch_shapes=[
            pltpu.VMEM(ocean.shape, F32),
            pltpu.VMEM(SEA, BF16),
            pltpu.VMEM(OWN, BF16),
            pltpu.VMEM(FAR, BF16),
            pltpu.VMEM((STEPS + 1, ocean.shape[2] + 2 * PAD, LANES), F32),
            pltpu.SemaphoreType.DMA((4,)),
        ]
        + atmos_scratch(chunks),
        input_output_aliases={10: 0},
        compiler_params=params(40),
        cost_estimate=cost(3 * 512 * 1024 * WIDE, 6),
        name="atmosphere_1",
    )(edge, atm, ocean, low, high, side, flux, own, halo, sea, half)


def masked(pair, i):
    return jnp.where(iota(pair.shape, 0) % GROUP == i, pair, 0.0)


def send_rows(states, start, next_ref, prev_ref):
    for offset, out_ref in ((-HALO, next_ref), (0, prev_ref)):
        both = jnp.concatenate([select_rows(state, offset) for state in states], axis=0)
        for c in range(both.shape[1] // LANES):
            chunk = both[:, c * LANES : (c + 1) * LANES].T.astype(BF16)
            out_ref[start + c * LANES : start + (c + 1) * LANES] = chunk


def pack_kernel(
    atm_ref, ocean_ref, next_ref, prev_ref, level_ref, x_ref, sea_state, few, sems
):
    chunks = sems.shape[0]
    width = WIDE // chunks
    cells = [pl.ds(n * width, width) for n in range(chunks)]
    copies = fetch([(atm_ref.at[:, :, c], x_ref.at[:, :, c]) for c in cells], sems)
    (arrival,) = fetch([(ocean_ref, sea_state)], few)
    arrival.wait()
    send_rows([sea_state[v].astype(BF16) for v in range(2)], WIDE, next_ref, prev_ref)
    for n, copy in enumerate(copies):
        copy.wait()
        lanes = slice(n * width, (n + 1) * width)
        states = [x_ref[v, :, lanes].astype(BF16) for v in range(2)]
        send_rows(states, n * width, next_ref, prev_ref)
        level_ref[:, :, lanes] = x_ref[:, 0:16, lanes]


def pack(atm, ocean, chunks=4):
    rows = jax.ShapeDtypeStruct((WIDE + ocean.shape[2], LANES), BF16)
    return pl.pallas_call(
        pack_kernel,
        in_specs=[HBM, HBM],
        out_specs=[VMEM] * 3,
        out_shape=[rows, rows, jax.ShapeDtypeStruct((2, 16, WIDE), F32)],
        scratch_shapes=[
            pltpu.VMEM(atm.shape, F32),
            pltpu.VMEM(ocean.shape, F32),
            pltpu.SemaphoreType.DMA((1,)),
            pltpu.SemaphoreType.DMA((chunks,)),
        ],
        compiler_params=params(24),
        cost_estimate=cost(1 << 28, 5),
        name="pack_halo",
    )(atm, ocean)


def forward_kernel(
    count_ref, owner_ref, block_ref, source_ref, level_ref, w_ref, out_ref, place_ref,
    tiles_ref, picked, contrib, left, sems,
):
    tiles = owner_ref.shape[1]
    per_row = WIDE // LANES
    size = tiles // sems.shape[0]
    some = [pl.ds(n * size, size) for n in range(sems.shape[0])]
    copies = fetch([(w_ref.at[t], tiles_ref.at[t]) for t in some], sems)

    source = source_ref[...]
    cell = (source & (per_row - 1)) * 16 + (source >> (per_row.bit_length() - 1))
    gather = onehot(iota((tiles, 256), 1).astype(F32) == column(cell.astype(F32)))
    for v in range(2):
        rounded = level_ref[v].astype(BF16)
        blocks = [rounded[:, b * LANES : (b + 1) * LANES] for b in range(per_row)]
        picked[v] = mxu(gather, jnp.concatenate(blocks, axis=0))
    owner = owner_ref[...].astype(F32)
    earlier = (column(owner) == owner) & (iota((tiles, tiles), 0) < iota((tiles, tiles), 1))
    rank = jnp.sum(jnp.where(earlier, 1.0, 0.0), axis=0, keepdims=True)
    live = iota((1, tiles), 1) < count_ref[0]
    place = jnp.where(live, owner_ref[...] * ROWS + rank.astype(jnp.int32), -64)
    index = jnp.where(live, owner_ref[...] * ROWS + 2 * CAP, -64)
    place_ref[0:1] = place
    place_ref[1:2] = jnp.where(live, cell, -64)
    place_ref[2:8] = jnp.zeros((6, tiles), jnp.int32)
    block = block_ref[...]
    lane = column(rank * 16.0 + ((block & 1) * 8 + (block >> 1)).astype(F32))
    names = onehot(iota((tiles, LANES), 1).astype(F32) == lane)
    part = out_ref.shape[0] // len(copies)

    for n, copy in enumerate(copies):
        copy.wait()
        row = iota((part, tiles), 0) + n * part
        here = slice(n * part, (n + 1) * part)
        for m, at in enumerate((place, place + CAP, index)):
            left[here, m * tiles : (m + 1) * tiles] = onehot(row == at)
        for t in range(n * size, (n + 1) * size, GROUP):
            rows = slice(t, t + GROUP)
            pair = jnp.concatenate([picked[0, rows], picked[1, rows]], axis=0)
            spread = jnp.concatenate([masked(pair, i).astype(BF16) for i in range(GROUP)], axis=1)
            both = mxu(spread, tiles_ref[rows].reshape(GROUP * LANES, LANES))
            contrib[0, rows] = both[:GROUP]
            contrib[1, rows] = both[GROUP:]

    first = jnp.concatenate(split(contrib[0]), axis=1)
    second = jnp.concatenate(split(contrib[1]), axis=1)
    third = jnp.concatenate([names, jnp.zeros_like(names)], axis=1)
    out = mxu(left[...], jnp.concatenate([first, second, third], axis=0))
    out_ref[...] = out[:, :LANES] + out[:, LANES:]


def forward(count, owner, block, source, level, weights, devices, parts=8):
    tiles = weights.shape[0]
    return pl.pallas_call(
        forward_kernel,
        in_specs=[SMEM, VMEM, VMEM, VMEM, VMEM, HBM],
        out_specs=[VMEM] * 2,
        out_shape=[
            jax.ShapeDtypeStruct((devices * ROWS, LANES), F32),
            jax.ShapeDtypeStruct((8, tiles), jnp.int32),
        ],
        scratch_shapes=[
            pltpu.VMEM(weights.shape, BF16),
            pltpu.VMEM((2, tiles, LANES), F32),
            pltpu.VMEM((2, tiles, LANES), F32),
            pltpu.VMEM((devices * ROWS, 3 * tiles), BF16),
            pltpu.SemaphoreType.DMA((parts,)),
        ],
        compiler_params=params(32),
        cost_estimate=cost(32 * tiles * LANES * LANES, 9),
        name="tiles_forward",
    )(count, owner, block, source, level, weights)


def combine_kernel(inbox_ref, ocean_ref, out_ref, flux_ref):
    devices = inbox_ref.shape[0] // ROWS

    def plane(r):
        return pl.ds(r, devices, stride=ROWS)

    names = inbox_ref[plane(6), :]
    parts = []
    for r in range(2 * CAP):
        value = inbox_ref[plane(r), :]
        high, low = split(value)
        rest = (value - high.astype(F32) - low.astype(F32)).astype(BF16)
        parts += [high, low, rest]
    summed = mxu(names.T.astype(BF16), jnp.concatenate(parts, axis=1))
    fields = []
    for v in range(2):
        received = 0.0
        for k in range(CAP):
            rows = summed[k * 16 : (k + 1) * 16]
            for term in range(3):
                at = ((v * CAP + k) * 3 + term) * LANES
                received = received + rows[:, at : at + LANES]
        surface = ocean_ref[v, 0:8]
        flux = received - jnp.concatenate([surface[:, :LANES], surface[:, LANES:]], axis=0)
        flux_ref[v] = jnp.concatenate([flux[:8], flux[8:]], axis=1)
        sent = flux.astype(BF16).astype(F32)
        empty = jnp.zeros_like(sent)
        for k in range(CAP):
            stack = [sent if j == k else empty for j in range(8)]
            fields.append(jnp.concatenate(stack, axis=0).astype(BF16))
    outgoing = mxu(names.astype(BF16), jnp.concatenate(fields, axis=1))
    for r in range(2 * CAP):
        out_ref[plane(r), :] = outgoing[:, r * LANES : (r + 1) * LANES]
    for r in range(2 * CAP, ROWS):
        out_ref[plane(r), :] = jnp.zeros((devices, LANES), F32)


def combine(inbox, ocean):
    return pl.pallas_call(
        combine_kernel,
        in_specs=[VMEM, VMEM],
        out_specs=[VMEM, VMEM],
        out_shape=[
            jax.ShapeDtypeStruct(inbox.shape, F32),
            jax.ShapeDtypeStruct((2, 8, 256), F32),
        ],
        compiler_params=params(24),
        name="ocean_flux",
    )(inbox, ocean)


def backward_kernel(
    place_ref, inbox_ref, w_ref, zero_ref, one_ref, _, out_ref,
    tiles_ref, picked, terms, held, sems, parts,
):
    tiles = place_ref.shape[1]
    size = tiles // parts.shape[0]
    some = [pl.ds(n * size, size) for n in range(parts.shape[0])]
    arrivals = fetch([(w_ref.at[t], tiles_ref.at[t]) for t in some], parts)
    per_row = WIDE // LANES
    place = column(place_ref[0:1].astype(F32)).astype(jnp.int32)
    inbox = inbox_ref[...].astype(BF16)
    slot = iota((tiles, inbox.shape[0]), 1)
    for v in range(2):
        picked[v] = mxu(onehot(slot == place + v * CAP), inbox)
    scatter = onehot(iota((256, tiles), 0) == place_ref[1:2])

    for t in range(0, tiles, GROUP):
        if t % size == 0:
            arrivals[t // size].wait()
        rows = slice(t, t + GROUP)
        pair = jnp.concatenate([picked[0, rows], picked[1, rows]], axis=0)
        weights = tiles_ref[rows].reshape(GROUP * LANES, LANES)
        wide = mxu(pair.astype(BF16), weights, ((1,), (1,)))
        both = 0.0
        for i in range(GROUP):
            both = both + masked(wide[:, i * LANES : (i + 1) * LANES], i)
        terms[0, rows] = both[:GROUP]
        terms[1, rows] = both[GROUP:]

    halves = [part for v in range(2) for part in split(terms[v])]
    summed = mxu(scatter, jnp.concatenate(halves, axis=1))
    copies = []
    for v, level_ref in enumerate((zero_ref, one_ref)):
        at = 2 * v * LANES
        returned = summed[:, at : at + LANES] + summed[:, at + LANES : at + 2 * LANES]
        for b in range(per_row):
            lanes = slice(b * LANES, (b + 1) * LANES)
            held[v, :, lanes] = level_ref[:, lanes] - couple * returned[b * 16 : (b + 1) * 16]
        copy = pltpu.make_async_copy(held.at[v], out_ref.at[v, pl.ds(0, 16)], sems.at[v])
        copy.start()
        copies.append(copy)
    for copy in copies:
        copy.wait()


def backward(place, inbox, weights, zero, one, atm, parts=8):
    tiles = weights.shape[0]
    return pl.pallas_call(
        backward_kernel,
        in_specs=[VMEM, VMEM, HBM, VMEM, VMEM, HBM],
        out_specs=HBM,
        out_shape=pltpu.HBM(atm.shape, F32),
        scratch_shapes=[
            pltpu.VMEM(weights.shape, BF16),
            pltpu.VMEM((2, tiles, LANES), F32),
            pltpu.VMEM((2, tiles, LANES), F32),
            pltpu.VMEM((2, 16, WIDE), F32),
            pltpu.SemaphoreType.DMA((2,)),
            pltpu.SemaphoreType.DMA((parts,)),
        ],
        input_output_aliases={5: 0},
        compiler_params=params(32),
        cost_estimate=cost(32 * tiles * LANES * LANES, 1),
        name="tiles_backward",
    )(place, inbox, weights, zero, one, atm)


def swap(rows):
    devices = lax.axis_size(RING)
    boxes = rows.reshape(devices, ROWS, LANES)
    return lax.all_to_all(boxes, RING, split_axis=0, concat_axis=0, tiled=True).reshape(rows.shape)


def per_device(
    atm_state,
    ocean_state,
    atm_levels,
    ocean_levels,
    tile_weight,
    tile_owner,
    tile_block,
    tile_source,
    tile_count,
):
    devices = lax.axis_size(RING)
    tiles = tile_weight.shape[0]
    atm = atm_state.reshape(2, 256, WIDE)
    ocean = ocean_state.reshape(2, 128, 256)
    grp, dom = lax.axis_index("grp"), lax.axis_index("dom")
    last = lax.axis_size("dom") - 1
    edge = jnp.stack([grp, (dom == 0).astype(jnp.int32), (dom == last).astype(jnp.int32)])

    atm = pltpu.with_memory_space_constraint(atm, pltpu.HBM)
    sea_state = pltpu.with_memory_space_constraint(ocean, pltpu.HBM)
    tile_weight = pltpu.with_memory_space_constraint(tile_weight, pltpu.HBM)
    lists = [x.reshape(1, tiles) for x in (tile_owner, tile_block, tile_source)]
    to_next, to_prev, level = pack(atm, sea_state)
    forth = [(i, (i + 1) % devices) for i in range(devices)]
    back = [(target, source) for source, target in forth]
    low = lax.ppermute(to_next, RING, forth)
    high = lax.ppermute(to_prev, RING, back)
    outbox, place = forward(tile_count, *lists, level, tile_weight, devices)
    inbox = swap(outbox)
    columns = edge_rows(edge, ocean, low, high)
    side = lax.ppermute(columns, "grp", [(0, 1), (1, 0)])
    half, zero, *operators = early(edge, atm_levels, ocean_levels, atm, low, high)
    operators = [pltpu.with_memory_space_constraint(x, pltpu.HBM) for x in operators]
    inbox, half, side = lax.optimization_barrier((inbox, half, side))
    outgoing, flux = combine(inbox, ocean)
    returned = swap(outgoing)
    whole, one, ocean_final = late(
        edge, atm, sea_state, low, high, side, flux, *operators, half
    )
    returned, whole, ocean_final = lax.optimization_barrier((returned, whole, ocean_final))
    atm_final = backward(place, returned, tile_weight, zero, one, whole)
    return atm_final.reshape(atm_state.shape), ocean_final.reshape(ocean_state.shape)


def solution(mesh):
    in_specs = (
        P(None, None, RING, None),
        P(None, None, "dom", "grp"),
        P(),
        P(),
        P(RING, None, None),
        P(RING, None),
        P(RING),
        P(RING),
        P(RING),
    )
    out_specs = (P(None, None, RING, None), P(None, None, "dom", "grp"))
    return jax.shard_map(
        per_device, mesh=mesh, in_specs=in_specs, out_specs=out_specs, check_vma=False
    )
```

profile of v0, /device:TPU:1, one launch (start us, length us, event | category | flops | bytes accessed | tf_op | source)
XLA Modules:
  0.0 66.2 jit_solution(8736240990490164404)
XLA Ops:
  0.6 0.0 copy-start.3
  0.6 0.0 copy-start.2
  0.7 0.0 copy-start.1
  0.7 4.0 %pack_halo.1 = (bf16[2304,128]{1,0:T(8,128)(2,1)S(1)}, bf16[2304,128]{1,0:T(8,128)(2,1)S(1)}, f32[2,16,2048]{2,1,0:T(8,128)S(1)}) custom-call(f32[2,256,2048]{2,1,0:T(8,128)} %bitcast.23, f32[2,128,256]{2,1,0:T(8,128)} %bitcast.14), custom_call_target="tpu_custom_call" | custom-call | flops 268435456 | bytes 5242880 | tf_op jit(solution)/shard_map/pack_halo/pallas_call | solution.py:484
  4.7 4.4 %collective-permute-start = (bf16[2304,128]{1,0:T(8,128)(2,1)S(1)}, bf16[2304,128]{1,0:T(8,128)(2,1)S(1)}, u32[]{:S(2)}, u32[]{:S(2)}) collective-permute-start(bf16[2304,128]{1,0:T(8,128)(2,1)S(1)} %get-tuple-element.26), channel_id=1, source_target_pairs={{0,1},{1,2},{2,3},{3,4},{4,5},{5,6},{6,7},{7,8},{8,9},{9,10},{10,1... | collective-permute-start | bytes 1769480 | tf_op jit(solution)/shard_map/ppermute | solution.py:726
  9.1 0.0 collective-permute-start.1
  9.7 0.0 copy-done.3
  9.8 0.0 copy-done.2
  9.8 0.0 copy-done.1
  9.8 0.0 copy-start
  9.8 0.0 copy-start.4
  9.8 0.0 copy-start.5
  9.8 5.2 %tiles_forward.1 = (f32[1024,128]{1,0:T(8,128)}, s32[8,256]{1,0:T(8,128)S(1)}) custom-call(s32[1]{0:T(128)S(6)} %copy.15.count_ref, s32[1,256]{1,0:T(1,128)S(1)} %bitcast.20, s32[1,256]{1,0:T(1,128)S(1)} %bitcast.21, s32[1,256]{1,0:T(1,128)S(1)} %bitcast.22, f32[2,16,2048]{2,1,0:T(8,128)S(1)} %get-tuple-element.23.level_ref, bf16[256,128,128]{2,1,0:T(8,128)(2,1)} %w_ref.3), custom_call_target="tpu_custom_call" | custom-call | flops 134217728 | bytes 9437184 | tf_op jit(solution)/shard_map/tiles_forward/pallas_call | solution.py:555
  15.0 10.4 %all-to-all-start = ((f32[128,8,128]{2,1,0:T(8,128)}), f32[128,8,128]{2,1,0:T(8,128)S(1)}, u32[]{:S(2)}, u32[]{:S(2)}) async-start(f32[128,8,128]{2,1,0:T(8,128)} %bitcast.5), calls=%async_computation | async-start | bytes 1048576 | tf_op jit(solution)/shard_map/all_to_all | solution.py:697
  25.5 0.1 pad_add_fusion.edge_ref
  25.5 0.0 collective-permute-done.low_ref
  25.5 0.0 collective-permute-done.1.high_ref
  25.5 0.0 copy-done
  25.5 0.6 ocean_edge.1
  26.2 1.5 %collective-permute-start.2 = (f32[32,128]{1,0:T(8,128)S(1)}, f32[32,128]{1,0:T(8,128)S(1)}, u32[]{:S(2)}, u32[]{:S(2)}) collective-permute-start(f32[32,128]{1,0:T(8,128)S(1)} %ocean_edge.1), channel_id=1, source_target_pairs={{0,64},{64,0},{1,65},{65,1},{2,66},{66,2},{3,67},{67,3},{4,68},{68... | collective-permute-start | bytes 49160 | tf_op jit(solution)/shard_map/ppermute | solution.py:731
  27.7 0.0 copy-done.4
  27.7 0.0 copy-done.5
  27.7 8.3 %atmosphere_0.1 = (f32[2,256,2048]{2,1,0:T(8,128)}, f32[16,2048]{1,0:T(8,128)S(1)}, bf16[768,512]{1,0:T(8,128)(2,1)}, bf16[128,1024]{1,0:T(8,128)(2,1)}, bf16[384,512]{1,0:T(8,128)(2,1)}) custom-call(s32[3]{0:T(128)S(1)} %pad_add_fusion.edge_ref, f32[16,16]{1,0:T(8,128)S(1)} %copy-done.4, f32[16,16]{1,0:T(8,128)S(1)} %copy-done.5, f32[2,256,2048]{2,1,0:T(8,128)} %bitcast.24, ...), custom_call_target="tpu_custom_call" | custom-call | flops 3221225472 | bytes 6291456 | tf_op jit(solution)/shard_map/atmosphere_0/pallas_call | solution.py:340
  36.0 3.2 %all-to-all-done = f32[128,8,128]{2,1,0:T(8,128)S(1)} async-done(((f32[128,8,128]{2,1,0:T(8,128)}), f32[128,8,128]{2,1,0:T(8,128)S(1)}, u32[]{:S(2)}, u32[]{:S(2)}) %all-to-all-start) | async-done | bytes 524320 | tf_op jit(solution)/shard_map/all_to_all | solution.py:697
  39.1 0.0 collective-permute-done.2.side_ref
  39.1 1.4 %ocean_flux.1 = (f32[1024,128]{1,0:T(8,128)}, f32[2,8,256]{2,1,0:T(8,128)S(1)}) custom-call(f32[1024,128]{1,0:T(8,128)S(1)} %bitcast.19, f32[2,128,256]{2,1,0:T(8,128)S(1)} %bitcast.17), custom_call_target="tpu_custom_call" | custom-call | tf_op jit(solution)/shard_map/ocean_flux/pallas_call | solution.py:614
  40.5 6.5 %all-to-all-start.1 = ((f32[128,8,128]{2,1,0:T(8,128)}), f32[128,8,128]{2,1,0:T(8,128)S(1)}, u32[]{:S(2)}, u32[]{:S(2)}) async-start(f32[128,8,128]{2,1,0:T(8,128)} %bitcast.10), calls=%async_computation.1 | async-start | bytes 1048576 | tf_op jit(solution)/shard_map/all_to_all | solution.py:697
  47.0 10.8 %atmosphere_1.1 = (f32[2,256,2048]{2,1,0:T(8,128)}, f32[16,2048]{1,0:T(8,128)S(1)}, f32[2,128,256]{2,1,0:T(8,128)}) custom-call(s32[3]{0:T(128)S(1)} %pad_add_fusion.edge_ref, f32[2,256,2048]{2,1,0:T(8,128)} %bitcast.25, f32[2,128,256]{2,1,0:T(8,128)} %bitcast.15, ...), custom_call_target="tpu_custom_call", output_to_operand_aliasing={{0}: (10, {})} | custom-call | flops 3221225472 | bytes 6291456 | tf_op jit(solution)/shard_map/atmosphere_1/pallas_call | solution.py:427
  57.7 2.9 %all-to-all-done.1 = f32[128,8,128]{2,1,0:T(8,128)S(1)} async-done(((f32[128,8,128]{2,1,0:T(8,128)}), f32[128,8,128]{2,1,0:T(8,128)S(1)}, u32[]{:S(2)}, u32[]{:S(2)}) %all-to-all-start.1) | async-done | bytes 524320 | tf_op jit(solution)/shard_map/all_to_all | solution.py:697
  60.6 5.5 %tiles_backward.1 = f32[2,256,2048]{2,1,0:T(8,128)} custom-call(s32[8,256]{1,0:T(8,128)S(1)} %get-tuple-element.24.place_ref, f32[1024,128]{1,0:T(8,128)S(1)} %bitcast.18, bf16[256,128,128]{2,1,0:T(8,128)(2,1)} %w_ref.3, f32[16,2048]{1,0:T(8,128)S(1)} %get-tuple-element.40.zero_ref, ...), custom_call_target="tpu_custom_call", output_to_operand_aliasing={{}: (5, {})} | custom-call | flops 134217728 | bytes 1048576 | tf_op jit(solution)/shard_map/tiles_backward/pallas_call | solution.py:674
Async XLA Ops:
  0.6 9.1 %copy-start.3 = (s32[256]{0:T(256)S(1)}, s32[256]{0:T(256)}, u32[]{:S(2)}) copy-start(s32[256]{0:T(256)} %param.16) | copy-start | bytes 3076
  0.6 9.1 %copy-start.2 = (s32[256]{0:T(256)S(1)}, s32[256]{0:T(256)}, u32[]{:S(2)}) copy-start(s32[256]{0:T(256)} %param.15) | copy-start | bytes 3076
  0.7 9.1 %copy-start.1 = (s32[256,1]{0,1:T(1,128)S(1)}, s32[256,1]{0,1:T(1,128)}, u32[]{:S(2)}) copy-start(s32[256,1]{0,1:T(1,128)} %param.14) | copy-start | bytes 3076
  4.7 20.8 %collective-permute-start = (bf16[2304,128]{1,0:T(8,128)(2,1)S(1)}, bf16[2304,128]{1,0:T(8,128)(2,1)S(1)}, u32[]{:S(2)}, u32[]{:S(2)}) collective-permute-start(bf16[2304,128]{1,0:T(8,128)(2,1)S(1)} %get-tuple-element.26), channel_id=1, source_target_pairs={{0,1},{1,2},{2,3},{3,4},{4,5},{5,6},{6,7},{7,8},{8,9},{9,10},{10,1... | collective-permute-start | bytes 1769480 | tf_op jit(solution)/shard_map/ppermute | solution.py:726
  9.1 16.4 %collective-permute-start.1 = (bf16[2304,128]{1,0:T(8,128)(2,1)S(1)}, bf16[2304,128]{1,0:T(8,128)(2,1)S(1)}, u32[]{:S(2)}, u32[]{:S(2)}) collective-permute-start(bf16[2304,128]{1,0:T(8,128)(2,1)S(1)} %get-tuple-element.27), channel_id=1, source_target_pairs={{1,0},{2,1},{3,2},{4,3},{5,4},{6,5},{7,6},{8,7},{9,8},{10,9},{11,1... | collective-permute-start | bytes 1769480 | tf_op jit(solution)/shard_map/ppermute | solution.py:727
  9.8 15.8 %copy-start = (f32[2,16,8,256]{3,2,1,0:T(8,128)S(1)}, f32[2,16,8,256]{3,2,1,0:T(8,128)}, u32[]{:S(2)}) copy-start(f32[2,16,8,256]{3,2,1,0:T(8,128)} %param.10) | copy-start | bytes 786436
  9.8 17.9 %copy-start.4 = (f32[16,16]{1,0:T(8,128)S(1)}, f32[16,16]{1,0:T(8,128)}, u32[]{:S(2)}) copy-start(f32[16,16]{1,0:T(8,128)} %atm_levels_ref.1) | copy-start | bytes 3076
  9.8 17.9 %copy-start.5 = (f32[16,16]{1,0:T(8,128)S(1)}, f32[16,16]{1,0:T(8,128)}, u32[]{:S(2)}) copy-start(f32[16,16]{1,0:T(8,128)} %ocean_levels_ref.1) | copy-start | bytes 3076
  15.0 24.1 %all-to-all-start = ((f32[128,8,128]{2,1,0:T(8,128)}), f32[128,8,128]{2,1,0:T(8,128)S(1)}, u32[]{:S(2)}, u32[]{:S(2)}) async-start(f32[128,8,128]{2,1,0:T(8,128)} %bitcast.5), calls=%async_computation | async-start | bytes 1048576 | tf_op jit(solution)/shard_map/all_to_all | solution.py:697
  26.2 12.9 %collective-permute-start.2 = (f32[32,128]{1,0:T(8,128)S(1)}, f32[32,128]{1,0:T(8,128)S(1)}, u32[]{:S(2)}, u32[]{:S(2)}) collective-permute-start(f32[32,128]{1,0:T(8,128)S(1)} %ocean_edge.1), channel_id=1, source_target_pairs={{0,64},{64,0},{1,65},{65,1},{2,66},{66,2},{3,67},{67,3},{4,68},{68... | collective-permute-start | bytes 49160 | tf_op jit(solution)/shard_map/ppermute | solution.py:731
  40.5 20.1 %all-to-all-start.1 = ((f32[128,8,128]{2,1,0:T(8,128)}), f32[128,8,128]{2,1,0:T(8,128)S(1)}, u32[]{:S(2)}, u32[]{:S(2)}) async-start(f32[128,8,128]{2,1,0:T(8,128)} %bitcast.10), calls=%async_computation.1 | async-start | bytes 1048576 | tf_op jit(solution)/shard_map/all_to_all | solution.py:697
where the time goes:
time: 66.5 us; the launch traced here: 66.2 us
  Pallas kernels  35.7 us (54%)
  starting transfers between devices  22.8 us (34%)
  waiting for transfers between devices  6.04 us (9%)
  between operations  1.59 us (2%)
    all_to_all x2, starting transfers between devices, swap(): lax.all_to_all(boxes, RING, split_axis=0, concat_axis=0, tiled=True)  16.9 us
    pallas_call x1, Pallas kernels, late(): pl.pallas_call(late_kernel, in_specs=[SMEM, HBM, HBM, VMEM, VMEM, VMEM, V...  10.8 us
    pallas_call x1, Pallas kernels, early(): pl.pallas_call(early_kernel, in_specs=[SMEM, VMEM, VMEM, HBM, VMEM, VMEM]...  8.27 us
    all_to_all x2, waiting for transfers between devices, swap(): lax.all_to_all(boxes, RING, split_axis=0, concat_axis=0, tiled=True)  6.03 us
    pallas_call x1, Pallas kernels, backward(): pl.pallas_call(backward_kernel, in_specs=[VMEM, VMEM, HBM, VMEM, VMEM, HB...  5.46 us
    pallas_call x1, Pallas kernels, forward(): pl.pallas_call(forward_kernel, in_specs=[SMEM, VMEM, VMEM, VMEM, VMEM, HB...  5.17 us
    ppermute x1, starting transfers between devices, per_device(): low = lax.ppermute(to_next, RING, forth)  4.37 us
    pallas_call x1, Pallas kernels, pack(): pl.pallas_call(pack_kernel, in_specs=[HBM, HBM], out_specs=[VMEM] * 3, ou...  4.05 us
  transfers between devices with their start and end apart: 5, of which 2 were waited for; matrix products, arithmetic and copies ran while one was open for 0% of the time, Pallas kernels for 38%

commit v1 on v0

--- a/solution.py
+++ b/solution.py
@@ -15,6 +15,7 @@
 LANES = 128
 GROUP = 8
 PAD = 8
+AHEAD = 64
 WIDE = 2048
 RING = ("grp", "dom")
 F32 = jnp.float32
@@ -77,11 +78,12 @@
     return jnp.sum(jnp.where(eye, jnp.broadcast_to(row, (n, n)), 0.0), axis=1, keepdims=True)
 
 
-def select_rows(state, offset):
+def select_rows(state):
     rows = state.shape[0]
     deep = rows // 16
-    out, col = iota((16 * HALO, rows), 0), iota((16 * HALO, rows), 1)
-    return mxu(onehot(col == (out >> 2) * deep + (out & 3) + offset % deep), state)
+    out, col = iota((32 * HALO, rows), 0), iota((32 * HALO, rows), 1)
+    first = ((out >> 2) & 15) * deep + (out & 3)
+    return mxu(onehot(col == jnp.where(out < 16 * HALO, first + deep - HALO, first)), state)
 
 
 def coefficients():
@@ -168,8 +170,8 @@
     return result
 
 
-def write_operators(edge_ref, levels, own_ref, halo_ref, ocean_ref):
-    for s, part in enumerate(operators(levels[0], 16, None)):
+def write_atmos(levels, own_ref, halo_ref):
+    for s, part in enumerate(operators(levels, 16, None)):
         high, low = split(part[:256])
         lanes = slice((s & 1) * 256, (s & 1) * 256 + 256)
         if s < 2:
@@ -178,8 +180,11 @@
         else:
             own_ref[512:768, lanes] = high
         halo_ref[:, s * 256 : (s + 1) * 256] = part[256:].astype(BF16)
+
+
+def write_ocean(edge_ref, levels, ocean_ref):
     image = (edge_ref[1], edge_ref[2])
-    for s, part in enumerate(operators(levels[1], 8, image)):
+    for s, part in enumerate(operators(levels, 8, image)):
         lanes = slice(s * LANES, (s + 1) * LANES)
         high, low = split(part[:128])
         ocean_ref[0:128, lanes] = low
@@ -292,7 +297,12 @@
 def fetch_atmos(v, atm_ref, x_ref, sems):
     size = WIDE // sems.shape[0]
     cells = [pl.ds(n * size, size) for n in range(sems.shape[0])]
-    return fetch([(atm_ref.at[v, :, c], x_ref.at[:, c]) for c in cells], sems)
+    copies = [
+        pltpu.make_async_copy(atm_ref.at[v, :, c], x_ref.at[:, c], sems.at[n])
+        for n, c in enumerate(cells)
+    ]
+    copies[0].start()
+    return copies
 
 
 def edge_kernel(edge_ref, ocean_ref, low_ref, high_ref, out_ref):
@@ -319,19 +329,21 @@
 
 def early_kernel(
     edge_ref, atm_levels_ref, ocean_levels_ref, atm_ref, low_ref, high_ref,
-    out_ref, surface_ref, own_out, halo_out, sea_out,
-    levels, own, halo, sea, few, *rest,
+    out_ref, surface_ref, halo, sea, own_out, levels, own, few, *rest,
 ):
     x_ref, x_sems = rest[:2]
     arrivals = fetch_atmos(0, atm_ref, x_ref, x_sems)
     levels[...] = jnp.zeros_like(levels)
     levels[0, 0:16, 0:16] = atm_levels_ref[...]
     levels[1, 0:16, 0:16] = ocean_levels_ref[...]
-    write_operators(edge_ref, (levels[0], levels[1]), own, halo, sea)
-    keep = fetch([(own, own_out), (halo, halo_out), (sea, sea_out)], few)
+    write_atmos(levels[0], own, halo)
+    for copy in arrivals[1:]:
+        copy.start()
+    keep = fetch([(own, own_out)], few)
     sent = atmos_steps(
         0, arrivals, x_ref, low_ref, high_ref, own, halo, out_ref, surface_ref, *rest[2:]
     )
+    write_ocean(edge_ref, levels[1], sea)
     for copy in keep + sent:
         copy.wait()
 
@@ -340,20 +352,18 @@
     return pl.pallas_call(
         early_kernel,
         in_specs=[SMEM, VMEM, VMEM, HBM, VMEM, VMEM],
-        out_specs=[HBM, VMEM, HBM, HBM, HBM],
+        out_specs=[HBM, VMEM, VMEM, VMEM, HBM],
         out_shape=[
             pltpu.HBM(atm.shape, F32),
             jax.ShapeDtypeStruct((16, WIDE), F32),
+            jax.ShapeDtypeStruct(FAR, BF16),
+            jax.ShapeDtypeStruct(SEA, BF16),
             pltpu.HBM(OWN, BF16),
-            pltpu.HBM(FAR, BF16),
-            pltpu.HBM(SEA, BF16),
         ],
         scratch_shapes=[
             pltpu.VMEM((2, LANES, LANES), F32),
             pltpu.VMEM(OWN, BF16),
-            pltpu.VMEM(FAR, BF16),
-            pltpu.VMEM(SEA, BF16),
-            pltpu.SemaphoreType.DMA((3,)),
+            pltpu.SemaphoreType.DMA((1,)),
         ]
         + atmos_scratch(chunks),
         compiler_params=params(40),
@@ -362,7 +372,7 @@
     )(edge, atm_levels, ocean_levels, atm, low, high)
 
 
-def ocean_steps(first, ocean_ref, low_ref, high_ref, side_ref, g_ref, flux_ref, out_ref, w):
+def ocean_steps(v, first, ocean_ref, low_ref, high_ref, side_ref, g_ref, flux_ref, out_ref, w):
     wide = ocean_ref.shape[2]
 
     def extend(rows, side):
@@ -374,59 +384,61 @@
     for n, ref in enumerate((low_ref, high_ref)):
         side = side_ref[(2 + n) * PAD : (3 + n) * PAD]
         halos.append(extend(ref[WIDE : WIDE + wide].astype(F32), side).astype(BF16))
-    for v in range(2):
-        own = jnp.concatenate([ocean_ref[v, :, :LANES].T, ocean_ref[v, :, LANES:].T], axis=0)
-        state = extend(own, side_ref[v * PAD : (v + 1) * PAD])
-        high, low = split(state)
-        left = jnp.concatenate([high, low, high] + halos, axis=1)
-        g = g_ref[...]
-        right = jnp.concatenate([g[:256], g[128:256], halo_rows(g[256:], v)], axis=0)
-        for s in range(STEPS):
-            w[s] = mxu(left, right[:, s * LANES : (s + 1) * LANES])
-        w[STEPS] = state * diffuse**STEPS
-        end = wide + PAD
+    own = jnp.concatenate([ocean_ref[v, :, :LANES].T, ocean_ref[v, :, LANES:].T], axis=0)
+    state = extend(own, side_ref[v * PAD : (v + 1) * PAD])
+    high, low = split(state)
+    left = jnp.concatenate([high, low, high] + halos, axis=1)
+    g = g_ref[...]
+    right = jnp.concatenate([g[:256], g[128:256], halo_rows(g[256:], v)], axis=0)
+    for s in range(0, STEPS, 2):
+        both = mxu(left, right[:, s * LANES : (s + 2) * LANES])
+        w[s], w[s + 1] = both[:, :LANES], both[:, LANES:]
+    w[STEPS] = state * diffuse**STEPS
+    end = wide + PAD
+    for s in range(1, STEPS + 1):
+        w[s, 0:PAD] = jnp.where(first, mirror_low(w[s, PAD : 2 * PAD]), w[s, 0:PAD])
+        w[s, end : end + PAD] = jnp.where(
+            first, w[s, end : end + PAD], mirror_high(w[s, end - PAD : end])
+        )
+    for c in range(wide // LANES):
+        at = PAD + c * LANES
+        total = w[0, at : at + LANES]
         for s in range(1, STEPS + 1):
-            w[s, 0:PAD] = jnp.where(first, mirror_low(w[s, PAD : 2 * PAD]), w[s, 0:PAD])
-            w[s, end : end + PAD] = jnp.where(
-                first, w[s, end : end + PAD], mirror_high(w[s, end - PAD : end])
-            )
-        for c in range(wide // LANES):
-            at = PAD + c * LANES
-            total = w[0, at : at + LANES]
-            for s in range(1, STEPS + 1):
-                total += w[s, at - s : at - s + LANES]
-                total += w[s, at + s : at + s + LANES]
-            final = total.T
-            lanes = slice(c * LANES, (c + 1) * LANES)
-            out_ref[v, :, lanes] = final
-            out_ref[v, 0:8, lanes] = final[0:8] + couple * flux_ref[v, :, lanes]
+            total += w[s, at - s : at - s + LANES]
+            total += w[s, at + s : at + s + LANES]
+        final = total.T
+        lanes = slice(c * LANES, (c + 1) * LANES)
+        out_ref[v, :, lanes] = final
+        out_ref[v, 0:8, lanes] = final[0:8] + couple * flux_ref[v, :, lanes]
 
 
 def late_kernel(
-    edge_ref, atm_ref, ocean_ref, low_ref, high_ref, side_ref, flux_ref, own_ref, halo_ref,
-    sea_ref, _, out_ref, surface_ref, ocean_out, state, sea, own, halo, sea_w, few, *rest,
+    edge_ref, atm_ref, ocean_ref, low_ref, high_ref, side_ref, flux_ref, halo_ref, sea_ref,
+    own_ref, _, out_ref, surface_ref, ocean_out, own, sea_w, few, *rest,
 ):
     x_ref, x_sems = rest[:2]
-    arrivals = fetch(
-        [(ocean_ref, state), (sea_ref, sea), (own_ref, own), (halo_ref, halo)], few
-    )
+    (arrival,) = fetch([(own_ref, own)], few)
     x_arrivals = fetch_atmos(1, atm_ref, x_ref, x_sems)
-    for copy in arrivals:
-        copy.wait()
-    ocean_steps(
-        edge_ref[0] == 0, state, low_ref, high_ref, side_ref, sea, flux_ref, ocean_out, sea_w
-    )
+    ocean = (
+        edge_ref[0] == 0, ocean_ref, low_ref, high_ref, side_ref, sea_ref, flux_ref, ocean_out,
+        sea_w,
+    )
+    ocean_steps(0, *ocean)
+    for copy in x_arrivals[1:]:
+        copy.start()
+    arrival.wait()
     sent = atmos_steps(
-        1, x_arrivals, x_ref, low_ref, high_ref, own, halo, out_ref, surface_ref, *rest[2:]
-    )
+        1, x_arrivals, x_ref, low_ref, high_ref, own, halo_ref, out_ref, surface_ref, *rest[2:]
+    )
+    ocean_steps(1, *ocean)
     for copy in sent:
         copy.wait()
 
 
-def late(edge, atm, ocean, low, high, side, flux, own, halo, sea, half, chunks=4):
+def late(edge, atm, ocean, low, high, side, flux, halo, sea, own, half, chunks=4):
     return pl.pallas_call(
         late_kernel,
-        in_specs=[SMEM, HBM, HBM, VMEM, VMEM, VMEM, VMEM] + [HBM] * 4,
+        in_specs=[SMEM, HBM] + [VMEM] * 7 + [HBM] * 2,
         out_specs=[HBM, VMEM, VMEM],
         out_shape=[
             pltpu.HBM(atm.shape, F32),
@@ -434,19 +446,16 @@
             jax.ShapeDtypeStruct(ocean.shape, F32),
         ],
         scratch_shapes=[
-            pltpu.VMEM(ocean.shape, F32),
-            pltpu.VMEM(SEA, BF16),
             pltpu.VMEM(OWN, BF16),
-            pltpu.VMEM(FAR, BF16),
             pltpu.VMEM((STEPS + 1, ocean.shape[2] + 2 * PAD, LANES), F32),
-            pltpu.SemaphoreType.DMA((4,)),
+            pltpu.SemaphoreType.DMA((1,)),
         ]
         + atmos_scratch(chunks),
         input_output_aliases={10: 0},
         compiler_params=params(40),
         cost_estimate=cost(3 * 512 * 1024 * WIDE, 6),
         name="atmosphere_1",
-    )(edge, atm, ocean, low, high, side, flux, own, halo, sea, half)
+    )(edge, atm, ocean, low, high, side, flux, halo, sea, own, half)
 
 
 def masked(pair, i):
@@ -454,21 +463,25 @@
 
 
 def send_rows(states, start, next_ref, prev_ref):
-    for offset, out_ref in ((-HALO, next_ref), (0, prev_ref)):
-        both = jnp.concatenate([select_rows(state, offset) for state in states], axis=0)
+    picked = [select_rows(state) for state in states]
+    half = 16 * HALO
+    for rows, out_ref in ((slice(0, half), next_ref), (slice(half, None), prev_ref)):
+        both = jnp.concatenate([part[rows] for part in picked], axis=0)
         for c in range(both.shape[1] // LANES):
             chunk = both[:, c * LANES : (c + 1) * LANES].T.astype(BF16)
             out_ref[start + c * LANES : start + (c + 1) * LANES] = chunk
 
 
 def pack_kernel(
-    atm_ref, ocean_ref, next_ref, prev_ref, level_ref, x_ref, sea_state, few, sems
+    atm_ref, ocean_ref, w_ref, next_ref, prev_ref, level_ref, ahead_ref, x_ref, sea_state, few, sems
 ):
     chunks = sems.shape[0]
     width = WIDE // chunks
     cells = [pl.ds(n * width, width) for n in range(chunks)]
+    (arrival,) = fetch([(ocean_ref, sea_state)], few)
     copies = fetch([(atm_ref.at[:, :, c], x_ref.at[:, :, c]) for c in cells], sems)
-    (arrival,) = fetch([(ocean_ref, sea_state)], few)
+    ahead = pltpu.make_async_copy(w_ref.at[pl.ds(0, AHEAD)], ahead_ref, few.at[1])
+    ahead.start()
     arrival.wait()
     send_rows([sea_state[v].astype(BF16) for v in range(2)], WIDE, next_ref, prev_ref)
     for n, copy in enumerate(copies):
@@ -477,36 +490,61 @@
         states = [x_ref[v, :, lanes].astype(BF16) for v in range(2)]
         send_rows(states, n * width, next_ref, prev_ref)
         level_ref[:, :, lanes] = x_ref[:, 0:16, lanes]
-
-
-def pack(atm, ocean, chunks=4):
+    ahead.wait()
+
+
+def pack(atm, ocean, weights, chunks=2):
     rows = jax.ShapeDtypeStruct((WIDE + ocean.shape[2], LANES), BF16)
     return pl.pallas_call(
         pack_kernel,
-        in_specs=[HBM, HBM],
-        out_specs=[VMEM] * 3,
-        out_shape=[rows, rows, jax.ShapeDtypeStruct((2, 16, WIDE), F32)],
+        in_specs=[HBM, HBM, HBM],
+        out_specs=[VMEM] * 4,
+        out_shape=[
+            rows,
+            rows,
+            jax.ShapeDtypeStruct((2, 16, WIDE), F32),
+            jax.ShapeDtypeStruct((AHEAD, LANES, LANES), BF16),
+        ],
         scratch_shapes=[
             pltpu.VMEM(atm.shape, F32),
             pltpu.VMEM(ocean.shape, F32),
-            pltpu.SemaphoreType.DMA((1,)),
+            pltpu.SemaphoreType.DMA((2,)),
             pltpu.SemaphoreType.DMA((chunks,)),
         ],
         compiler_params=params(24),
         cost_estimate=cost(1 << 28, 5),
         name="pack_halo",
-    )(atm, ocean)
+    )(atm, ocean, weights)
+
+
+def fetch_tiles(w_ref, tiles_ref, sems):
+    count = tiles_ref.shape[0]
+    first, size = w_ref.shape[0] - count, count // sems.shape[0]
+    starts = [n * size for n in range(sems.shape[0])]
+    return fetch(
+        [(w_ref.at[pl.ds(first + t, size)], tiles_ref.at[pl.ds(t, size)]) for t in starts], sems
+    )
+
+
+def held_tiles(t, ahead_ref, tiles_ref, copies):
+    ahead = 0 if ahead_ref is None else ahead_ref.shape[0]
+    if t < ahead:
+        held = ahead_ref[t : t + GROUP]
+    else:
+        size = tiles_ref.shape[0] // len(copies)
+        if (t - ahead) % size == 0:
+            copies[(t - ahead) // size].wait()
+        held = tiles_ref[t - ahead : t - ahead + GROUP]
+    return held.reshape(GROUP * LANES, LANES)
 
 
 def forward_kernel(
-    count_ref, owner_ref, block_ref, source_ref, level_ref, w_ref, out_ref, place_ref,
+    count_ref, owner_ref, block_ref, source_ref, level_ref, ahead_ref, w_ref, out_ref, place_ref,
     tiles_ref, picked, contrib, left, sems,
 ):
     tiles = owner_ref.shape[1]
     per_row = WIDE // LANES
-    size = tiles // sems.shape[0]
-    some = [pl.ds(n * size, size) for n in range(sems.shape[0])]
-    copies = fetch([(w_ref.at[t], tiles_ref.at[t]) for t in some], sems)
+    copies = fetch_tiles(w_ref, tiles_ref, sems)
 
     source = source_ref[...]
     cell = (source & (per_row - 1)) * 16 + (source >> (per_row.bit_length() - 1))
@@ -518,7 +556,7 @@
     owner = owner_ref[...].astype(F32)
     earlier = (column(owner) == owner) & (iota((tiles, tiles), 0) < iota((tiles, tiles), 1))
     rank = jnp.sum(jnp.where(earlier, 1.0, 0.0), axis=0, keepdims=True)
-    live = iota((1, tiles), 1) < count_ref[0]
+    live = iota((1, tiles), 1) < count_ref[...]
     place = jnp.where(live, owner_ref[...] * ROWS + rank.astype(jnp.int32), -64)
     index = jnp.where(live, owner_ref[...] * ROWS + 2 * CAP, -64)
     place_ref[0:1] = place
@@ -527,21 +565,20 @@
     block = block_ref[...]
     lane = column(rank * 16.0 + ((block & 1) * 8 + (block >> 1)).astype(F32))
     names = onehot(iota((tiles, LANES), 1).astype(F32) == lane)
-    part = out_ref.shape[0] // len(copies)
-
-    for n, copy in enumerate(copies):
-        copy.wait()
-        row = iota((part, tiles), 0) + n * part
-        here = slice(n * part, (n + 1) * part)
+    part = out_ref.shape[0] * GROUP // tiles
+
+    for t in range(0, tiles, GROUP):
+        held = held_tiles(t, ahead_ref, tiles_ref, copies)
+        row = iota((part, tiles), 0) + t // GROUP * part
+        here = slice(t // GROUP * part, (t // GROUP + 1) * part)
         for m, at in enumerate((place, place + CAP, index)):
             left[here, m * tiles : (m + 1) * tiles] = onehot(row == at)
-        for t in range(n * size, (n + 1) * size, GROUP):
-            rows = slice(t, t + GROUP)
-            pair = jnp.concatenate([picked[0, rows], picked[1, rows]], axis=0)
-            spread = jnp.concatenate([masked(pair, i).astype(BF16) for i in range(GROUP)], axis=1)
-            both = mxu(spread, tiles_ref[rows].reshape(GROUP * LANES, LANES))
-            contrib[0, rows] = both[:GROUP]
-            contrib[1, rows] = both[GROUP:]
+        rows = slice(t, t + GROUP)
+        pair = jnp.concatenate([picked[0, rows], picked[1, rows]], axis=0)
+        spread = jnp.concatenate([masked(pair, i).astype(BF16) for i in range(GROUP)], axis=1)
+        both = mxu(spread, held)
+        contrib[0, rows] = both[:GROUP]
+        contrib[1, rows] = both[GROUP:]
 
     first = jnp.concatenate(split(contrib[0]), axis=1)
     second = jnp.concatenate(split(contrib[1]), axis=1)
@@ -550,18 +587,18 @@
     out_ref[...] = out[:, :LANES] + out[:, LANES:]
 
 
-def forward(count, owner, block, source, level, weights, devices, parts=8):
+def forward(count, owner, block, source, level, ahead, weights, devices, parts=4):
     tiles = weights.shape[0]
     return pl.pallas_call(
         forward_kernel,
-        in_specs=[SMEM, VMEM, VMEM, VMEM, VMEM, HBM],
+        in_specs=[VMEM] * 6 + [HBM],
         out_specs=[VMEM] * 2,
         out_shape=[
             jax.ShapeDtypeStruct((devices * ROWS, LANES), F32),
             jax.ShapeDtypeStruct((8, tiles), jnp.int32),
         ],
         scratch_shapes=[
-            pltpu.VMEM(weights.shape, BF16),
+            pltpu.VMEM((tiles - AHEAD, LANES, LANES), BF16),
             pltpu.VMEM((2, tiles, LANES), F32),
             pltpu.VMEM((2, tiles, LANES), F32),
             pltpu.VMEM((devices * ROWS, 3 * tiles), BF16),
@@ -570,10 +607,10 @@
         compiler_params=params(32),
         cost_estimate=cost(32 * tiles * LANES * LANES, 9),
         name="tiles_forward",
-    )(count, owner, block, source, level, weights)
-
-
-def combine_kernel(inbox_ref, ocean_ref, out_ref, flux_ref):
+    )(count, owner, block, source, level, ahead, weights)
+
+
+def combine_kernel(inbox_ref, ocean_ref, out_ref, flux_ref, boxes):
     devices = inbox_ref.shape[0] // ROWS
 
     def plane(r):
@@ -605,9 +642,10 @@
             fields.append(jnp.concatenate(stack, axis=0).astype(BF16))
     outgoing = mxu(names.astype(BF16), jnp.concatenate(fields, axis=1))
     for r in range(2 * CAP):
-        out_ref[plane(r), :] = outgoing[:, r * LANES : (r + 1) * LANES]
+        boxes[plane(r), :] = outgoing[:, r * LANES : (r + 1) * LANES]
     for r in range(2 * CAP, ROWS):
-        out_ref[plane(r), :] = jnp.zeros((devices, LANES), F32)
+        boxes[plane(r), :] = jnp.zeros((devices, LANES), F32)
+    out_ref[...] = boxes[...].astype(BF16)
 
 
 def combine(inbox, ocean):
@@ -616,9 +654,10 @@
         in_specs=[VMEM, VMEM],
         out_specs=[VMEM, VMEM],
         out_shape=[
-            jax.ShapeDtypeStruct(inbox.shape, F32),
+            jax.ShapeDtypeStruct(inbox.shape, BF16),
             jax.ShapeDtypeStruct((2, 8, 256), F32),
         ],
+        scratch_shapes=[pltpu.VMEM(inbox.shape, F32)],
         compiler_params=params(24),
         name="ocean_flux",
     )(inbox, ocean)
@@ -629,23 +668,19 @@
     tiles_ref, picked, terms, held, sems, parts,
 ):
     tiles = place_ref.shape[1]
-    size = tiles // parts.shape[0]
-    some = [pl.ds(n * size, size) for n in range(parts.shape[0])]
-    arrivals = fetch([(w_ref.at[t], tiles_ref.at[t]) for t in some], parts)
+    arrivals = fetch_tiles(w_ref, tiles_ref, parts)
     per_row = WIDE // LANES
     place = column(place_ref[0:1].astype(F32)).astype(jnp.int32)
-    inbox = inbox_ref[...].astype(BF16)
+    inbox = inbox_ref[...]
     slot = iota((tiles, inbox.shape[0]), 1)
     for v in range(2):
         picked[v] = mxu(onehot(slot == place + v * CAP), inbox)
     scatter = onehot(iota((256, tiles), 0) == place_ref[1:2])
 
     for t in range(0, tiles, GROUP):
-        if t % size == 0:
-            arrivals[t // size].wait()
+        weights = held_tiles(t, None, tiles_ref, arrivals)
         rows = slice(t, t + GROUP)
         pair = jnp.concatenate([picked[0, rows], picked[1, rows]], axis=0)
-        weights = tiles_ref[rows].reshape(GROUP * LANES, LANES)
         wide = mxu(pair.astype(BF16), weights, ((1,), (1,)))
         both = 0.0
         for i in range(GROUP):
@@ -669,7 +704,7 @@
         copy.wait()
 
 
-def backward(place, inbox, weights, zero, one, atm, parts=8):
+def backward(place, inbox, weights, zero, one, atm, parts=4):
     tiles = weights.shape[0]
     return pl.pallas_call(
         backward_kernel,
@@ -720,22 +755,24 @@
     sea_state = pltpu.with_memory_space_constraint(ocean, pltpu.HBM)
     tile_weight = pltpu.with_memory_space_constraint(tile_weight, pltpu.HBM)
     lists = [x.reshape(1, tiles) for x in (tile_owner, tile_block, tile_source)]
-    to_next, to_prev, level = pack(atm, sea_state)
+    to_next, to_prev, level, ahead = pack(atm, sea_state, tile_weight)
     forth = [(i, (i + 1) % devices) for i in range(devices)]
     back = [(target, source) for source, target in forth]
     low = lax.ppermute(to_next, RING, forth)
     high = lax.ppermute(to_prev, RING, back)
-    outbox, place = forward(tile_count, *lists, level, tile_weight, devices)
+    outbox, place = forward(
+        tile_count.reshape(1, 1), *lists, level, ahead, tile_weight, devices
+    )
     inbox = swap(outbox)
     columns = edge_rows(edge, ocean, low, high)
     side = lax.ppermute(columns, "grp", [(0, 1), (1, 0)])
-    half, zero, *operators = early(edge, atm_levels, ocean_levels, atm, low, high)
-    operators = [pltpu.with_memory_space_constraint(x, pltpu.HBM) for x in operators]
+    half, zero, halo, sea, own = early(edge, atm_levels, ocean_levels, atm, low, high)
+    own = pltpu.with_memory_space_constraint(own, pltpu.HBM)
     inbox, half, side = lax.optimization_barrier((inbox, half, side))
     outgoing, flux = combine(inbox, ocean)
     returned = swap(outgoing)
     whole, one, ocean_final = late(
-        edge, atm, sea_state, low, high, side, flux, *operators, half
+        edge, atm, ocean, low, high, side, flux, halo, sea, own, half
     )
     returned, whole, ocean_final = lax.optimization_barrier((returned, whole, ocean_final))
     atm_final = backward(place, returned, tile_weight, zero, one, whole)

time: 66.5 us -> 62.7 us (0.943)
  Pallas kernels: 35.7 us -> 32.7 us
  waiting for transfers between devices: 6.04 us -> 5.36 us
    pallas_call x3, Pallas kernels: 20 us -> 17 us  [the longest x1 8.99 us: late(): pl.pallas_call(late_kernel, in_specs=[SMEM, HBM] + [VMEM] * 7 + [HBM] * 2...]
    all_to_all x2, waiting for transfers between devices: 6.03 us -> 5.35 us  [swap(): lax.all_to_all(boxes, RING, split_axis=0, concat_axis=0, tiled=True)]
  transfers between devices with their start and end apart: 5 -> 5, of which waited for: 2 -> 2; matrix products, arithmetic and copies ran while one was open for 0% -> 0% of each run, Pallas kernels for 38% -> 37%
where the time goes in v1:
time: 62.7 us; the launch traced here: 62.4 us
  Pallas kernels  32.7 us (52%)
  starting transfers between devices  22.6 us (36%)
  waiting for transfers between devices  5.36 us (9%)
  between operations  1.59 us (3%)
    all_to_all x2, starting transfers between devices, swap(): lax.all_to_all(boxes, RING, split_axis=0, concat_axis=0, tiled=True)  16.8 us
    pallas_call x1, Pallas kernels, late(): pl.pallas_call(late_kernel, in_specs=[SMEM, HBM] + [VMEM] * 7 + [HBM] * 2...  8.99 us
    pallas_call x1, Pallas kernels, early(): pl.pallas_call(early_kernel, in_specs=[SMEM, VMEM, VMEM, HBM, VMEM, VMEM]...  8.15 us
    pallas_call x1, Pallas kernels, backward(): pl.pallas_call(backward_kernel, in_specs=[VMEM, VMEM, HBM, VMEM, VMEM, HB...  5.6 us
    all_to_all x2, waiting for transfers between devices, swap(): lax.all_to_all(boxes, RING, split_axis=0, concat_axis=0, tiled=True)  5.35 us
    pallas_call x1, Pallas kernels, forward(): pl.pallas_call(forward_kernel, in_specs=[VMEM] * 6 + [HBM], out_specs=[VM...  5.03 us
    ppermute x1, starting transfers between devices, per_device(): low = lax.ppermute(to_next, RING, forth)  4.37 us
    pallas_call x1, Pallas kernels, pack(): pl.pallas_call(pack_kernel, in_specs=[HBM, HBM, HBM], out_specs=[VMEM] *...  3 us
  transfers between devices with their start and end apart: 5, of which 2 were waited for; matrix products, arithmetic and copies ran while one was open for 0% of the time, Pallas kernels for 37%

profile of v1, /device:TPU:1, one launch (start us, length us, event | category | flops | bytes accessed | tf_op | source)
XLA Modules:
  0.0 62.4 jit_solution(1481142771455438244)
XLA Ops:
  0.6 0.0 copy-start.1
  0.6 0.0 copy-start.2
  0.7 0.0 copy-start.3
  0.7 3.0 %pack_halo.1 = (bf16[2304,128]{1,0:T(8,128)(2,1)S(1)}, bf16[2304,128]{1,0:T(8,128)(2,1)S(1)}, f32[2,16,2048]{2,1,0:T(8,128)S(1)}, bf16[64,128,128]{2,1,0:T(8,128)(2,1)S(1)}) custom-call(f32[2,256,2048]{2,1,0:T(8,128)} %bitcast.25, f32[2,128,256]{2,1,0:T(8,128)} %bitcast.16, bf16[256,128,128]{2,1,0:T(8,128)(2,1)} %w_ref.5), custom_call_target="tpu_custom_call" | custom-call | flops 268435456 | bytes 5242880 | tf_op jit(solution)/shard_map/pack_halo/pallas_call | solution.py:498
  3.7 4.4 %collective-permute-start = (bf16[2304,128]{1,0:T(8,128)(2,1)S(1)}, bf16[2304,128]{1,0:T(8,128)(2,1)S(1)}, u32[]{:S(2)}, u32[]{:S(2)}) collective-permute-start(bf16[2304,128]{1,0:T(8,128)(2,1)S(1)} %get-tuple-element.28), channel_id=1, source_target_pairs={{0,1},{1,2},{2,3},{3,4},{4,5},{5,6},{6,7},{7,8},{8,9},{9,10},{10,1... | collective-permute-start | bytes 1769480 | tf_op jit(solution)/shard_map/ppermute | solution.py:761
  8.0 0.0 collective-permute-start.1
  8.7 0.0 copy-done.1
  8.7 0.0 copy-done.2
  8.7 0.0 copy-done.3
  8.7 0.0 copy-start
  8.7 0.0 copy-start.4
  8.8 0.0 copy-start.5
  8.8 5.0 %tiles_forward.1 = (f32[1024,128]{1,0:T(8,128)}, s32[8,256]{1,0:T(8,128)S(1)}) custom-call(s32[1,1]{1,0:T(1,128)} %bitcast.15.count_ref, s32[1,256]{1,0:T(1,128)S(1)} %bitcast.22, s32[1,256]{1,0:T(1,128)S(1)} %bitcast.23, s32[1,256]{1,0:T(1,128)S(1)} %bitcast.24, f32[2,16,2048]{2,1,0:T(8,128)S(1)} %get-tuple-element.24.level_ref, ...), custom_call_target="tpu_custom_call" | custom-call | flops 134217728 | bytes 9437184 | tf_op jit(solution)/shard_map/tiles_forward/pallas_call | solution.py:592
  13.8 10.4 %all-to-all-start = ((f32[128,8,128]{2,1,0:T(8,128)}), f32[128,8,128]{2,1,0:T(8,128)S(1)}, u32[]{:S(2)}, u32[]{:S(2)}) async-start(f32[128,8,128]{2,1,0:T(8,128)} %bitcast.6), calls=%async_computation | async-start | bytes 1048576 | tf_op jit(solution)/shard_map/all_to_all | solution.py:732
  24.3 0.1 pad_add_fusion.edge_ref
  24.3 0.0 collective-permute-done.low_ref
  24.3 0.0 collective-permute-done.1.high_ref
  24.3 0.0 copy-done
  24.3 0.6 %ocean_edge.1 = f32[32,128]{1,0:T(8,128)S(1)} custom-call(s32[3]{0:T(128)S(1)} %pad_add_fusion.edge_ref, f32[2,128,256]{2,1,0:T(8,128)S(1)} %bitcast.17, bf16[2304,128]{1,0:T(8,128)(2,1)S(1)} %collective-permute-done.low_ref, bf16[2304,128]{1,0:T(8,128)(2,1)S(1)} %collective-permute-done.1.high_ref), custom_call_target="tpu_custom_call" | custom-call | tf_op jit(solution)/shard_map/ocean_edge/pallas_call | solution.py:320
  25.0 1.5 %collective-permute-start.2 = (f32[32,128]{1,0:T(8,128)S(1)}, f32[32,128]{1,0:T(8,128)S(1)}, u32[]{:S(2)}, u32[]{:S(2)}) collective-permute-start(f32[32,128]{1,0:T(8,128)S(1)} %ocean_edge.1), channel_id=1, source_target_pairs={{0,64},{64,0},{1,65},{65,1},{2,66},{66,2},{3,67},{67,3},{4,68},{68... | collective-permute-start | bytes 49160 | tf_op jit(solution)/shard_map/ppermute | solution.py:768
  26.5 0.0 copy-done.4
  26.5 0.0 copy-done.5
  26.5 8.1 %atmosphere_0.1 = (f32[2,256,2048]{2,1,0:T(8,128)}, f32[16,2048]{1,0:T(8,128)S(1)}, bf16[128,1024]{1,0:T(8,128)(2,1)S(1)}, bf16[384,512]{1,0:T(8,128)(2,1)S(1)}, bf16[768,512]{1,0:T(8,128)(2,1)}) custom-call(s32[3]{0:T(128)S(1)} %pad_add_fusion.edge_ref, f32[16,16]{1,0:T(8,128)S(1)} %copy-done.4, f32[16,16]{1,0:T(8,128)S(1)} %copy-done.5, ...), custom_call_target="tpu_custom_call" | custom-call | flops 3221225472 | bytes 6291456 | tf_op jit(solution)/shard_map/atmosphere_0/pallas_call | solution.py:352
  34.6 3.3 %all-to-all-done = f32[128,8,128]{2,1,0:T(8,128)S(1)} async-done(((f32[128,8,128]{2,1,0:T(8,128)}), f32[128,8,128]{2,1,0:T(8,128)S(1)}, u32[]{:S(2)}, u32[]{:S(2)}) %all-to-all-start) | async-done | bytes 524320 | tf_op jit(solution)/shard_map/all_to_all | solution.py:732
  37.9 0.0 collective-permute-done.2.side_ref
  37.9 1.3 %ocean_flux.1 = (bf16[1024,128]{1,0:T(8,128)(2,1)}, f32[2,8,256]{2,1,0:T(8,128)S(1)}) custom-call(f32[1024,128]{1,0:T(8,128)S(1)} %bitcast.20, f32[2,128,256]{2,1,0:T(8,128)S(1)} %bitcast.18), custom_call_target="tpu_custom_call" | custom-call | tf_op jit(solution)/shard_map/ocean_flux/pallas_call | solution.py:652
  39.2 6.4 %all-to-all-start.1 = ((bf16[128,8,128]{2,1,0:T(8,128)(2,1)}), bf16[128,8,128]{2,1,0:T(8,128)(2,1)S(1)}, u32[]{:S(2)}, u32[]{:S(2)}) async-start(bf16[128,8,128]{2,1,0:T(8,128)(2,1)} %bitcast.11), calls=%async_computation.1 | async-start | bytes 524288 | tf_op jit(solution)/shard_map/all_to_all | solution.py:732
  45.6 9.0 %atmosphere_1.1 = (f32[2,256,2048]{2,1,0:T(8,128)}, f32[16,2048]{1,0:T(8,128)S(1)}, f32[2,128,256]{2,1,0:T(8,128)}) custom-call(s32[3]{0:T(128)S(1)} %pad_add_fusion.edge_ref, f32[2,256,2048]{2,1,0:T(8,128)} %bitcast.27, f32[2,128,256]{2,1,0:T(8,128)S(1)} %bitcast.19, ...), custom_call_target="tpu_custom_call", output_to_operand_aliasing={{0}: (10, {})} | custom-call | flops 3221225472 | bytes 6291456 | tf_op jit(solution)/shard_map/atmosphere_1/pallas_call | solution.py:439
  54.6 2.1 %all-to-all-done.1 = bf16[128,8,128]{2,1,0:T(8,128)(2,1)S(1)} async-done(((bf16[128,8,128]{2,1,0:T(8,128)(2,1)}), bf16[128,8,128]{2,1,0:T(8,128)(2,1)S(1)}, u32[]{:S(2)}, u32[]{:S(2)}) %all-to-all-start.1) | async-done | bytes 262176 | tf_op jit(solution)/shard_map/all_to_all | solution.py:732
  56.6 5.6 %tiles_backward.1 = f32[2,256,2048]{2,1,0:T(8,128)} custom-call(s32[8,256]{1,0:T(8,128)S(1)} %get-tuple-element.26.place_ref, bf16[1024,128]{1,0:T(8,128)(2,1)S(1)} %bitcast.21, bf16[256,128,128]{2,1,0:T(8,128)(2,1)} %w_ref.5, f32[16,2048]{1,0:T(8,128)S(1)} %get-tuple-element.42.zero_ref, ...), custom_call_target="tpu_custom_call", output_to_operand_aliasing={{}: (5, {})} | custom-call | flops 134217728 | bytes 1048576 | tf_op jit(solution)/shard_map/tiles_backward/pallas_call | solution.py:709
Async XLA Ops:
  0.6 8.1 %copy-start.1 = (s32[256,1]{0,1:T(1,128)S(1)}, s32[256,1]{0,1:T(1,128)}, u32[]{:S(2)}) copy-start(s32[256,1]{0,1:T(1,128)} %param.14) | copy-start | bytes 3076
  0.6 8.1 %copy-start.2 = (s32[256]{0:T(256)S(1)}, s32[256]{0:T(256)}, u32[]{:S(2)}) copy-start(s32[256]{0:T(256)} %param.15) | copy-start | bytes 3076
  0.7 8.1 %copy-start.3 = (s32[256]{0:T(256)S(1)}, s32[256]{0:T(256)}, u32[]{:S(2)}) copy-start(s32[256]{0:T(256)} %param.16) | copy-start | bytes 3076
  3.7 20.7 %collective-permute-start = (bf16[2304,128]{1,0:T(8,128)(2,1)S(1)}, bf16[2304,128]{1,0:T(8,128)(2,1)S(1)}, u32[]{:S(2)}, u32[]{:S(2)}) collective-permute-start(bf16[2304,128]{1,0:T(8,128)(2,1)S(1)} %get-tuple-element.28), channel_id=1, source_target_pairs={{0,1},{1,2},{2,3},{3,4},{4,5},{5,6},{6,7},{7,8},{8,9},{9,10},{10,1... | collective-permute-start | bytes 1769480 | tf_op jit(solution)/shard_map/ppermute | solution.py:761
  8.0 16.3 %collective-permute-start.1 = (bf16[2304,128]{1,0:T(8,128)(2,1)S(1)}, bf16[2304,128]{1,0:T(8,128)(2,1)S(1)}, u32[]{:S(2)}, u32[]{:S(2)}) collective-permute-start(bf16[2304,128]{1,0:T(8,128)(2,1)S(1)} %get-tuple-element.29), channel_id=1, source_target_pairs={{1,0},{2,1},{3,2},{4,3},{5,4},{6,5},{7,6},{8,7},{9,8},{10,9},{11,1... | collective-permute-start | bytes 1769480 | tf_op jit(solution)/shard_map/ppermute | solution.py:762
  8.7 15.6 %copy-start = (f32[2,16,8,256]{3,2,1,0:T(8,128)S(1)}, f32[2,16,8,256]{3,2,1,0:T(8,128)}, u32[]{:S(2)}) copy-start(f32[2,16,8,256]{3,2,1,0:T(8,128)} %param.10) | copy-start | bytes 786436
  8.7 17.7 %copy-start.4 = (f32[16,16]{1,0:T(8,128)S(1)}, f32[16,16]{1,0:T(8,128)}, u32[]{:S(2)}) copy-start(f32[16,16]{1,0:T(8,128)} %atm_levels_ref.1) | copy-start | bytes 3076
  8.8 17.7 %copy-start.5 = (f32[16,16]{1,0:T(8,128)S(1)}, f32[16,16]{1,0:T(8,128)}, u32[]{:S(2)}) copy-start(f32[16,16]{1,0:T(8,128)} %ocean_levels_ref.1) | copy-start | bytes 3076
  13.8 24.1 %all-to-all-start = ((f32[128,8,128]{2,1,0:T(8,128)}), f32[128,8,128]{2,1,0:T(8,128)S(1)}, u32[]{:S(2)}, u32[]{:S(2)}) async-start(f32[128,8,128]{2,1,0:T(8,128)} %bitcast.6), calls=%async_computation | async-start | bytes 1048576 | tf_op jit(solution)/shard_map/all_to_all | solution.py:732
  25.0 12.9 %collective-permute-start.2 = (f32[32,128]{1,0:T(8,128)S(1)}, f32[32,128]{1,0:T(8,128)S(1)}, u32[]{:S(2)}, u32[]{:S(2)}) collective-permute-start(f32[32,128]{1,0:T(8,128)S(1)} %ocean_edge.1), channel_id=1, source_target_pairs={{0,64},{64,0},{1,65},{65,1},{2,66},{66,2},{3,67},{67,3},{4,68},{68... | collective-permute-start | bytes 49160 | tf_op jit(solution)/shard_map/ppermute | solution.py:768
  39.2 17.4 %all-to-all-start.1 = ((bf16[128,8,128]{2,1,0:T(8,128)(2,1)}), bf16[128,8,128]{2,1,0:T(8,128)(2,1)S(1)}, u32[]{:S(2)}, u32[]{:S(2)}) async-start(bf16[128,8,128]{2,1,0:T(8,128)(2,1)} %bitcast.11), calls=%async_computation.1 | async-start | bytes 524288 | tf_op jit(solution)/shard_map/all_to_all | solution.py:732

commit v2 on v1

--- a/solution.py
+++ b/solution.py
@@ -473,15 +473,13 @@
 
 
 def pack_kernel(
-    atm_ref, ocean_ref, w_ref, next_ref, prev_ref, level_ref, ahead_ref, x_ref, sea_state, few, sems
+    atm_ref, ocean_ref, next_ref, prev_ref, level_ref, x_ref, sea_state, few, sems
 ):
     chunks = sems.shape[0]
     width = WIDE // chunks
     cells = [pl.ds(n * width, width) for n in range(chunks)]
     (arrival,) = fetch([(ocean_ref, sea_state)], few)
     copies = fetch([(atm_ref.at[:, :, c], x_ref.at[:, :, c]) for c in cells], sems)
-    ahead = pltpu.make_async_copy(w_ref.at[pl.ds(0, AHEAD)], ahead_ref, few.at[1])
-    ahead.start()
     arrival.wait()
     send_rows([sea_state[v].astype(BF16) for v in range(2)], WIDE, next_ref, prev_ref)
     for n, copy in enumerate(copies):
@@ -490,31 +488,29 @@
         states = [x_ref[v, :, lanes].astype(BF16) for v in range(2)]
         send_rows(states, n * width, next_ref, prev_ref)
         level_ref[:, :, lanes] = x_ref[:, 0:16, lanes]
-    ahead.wait()
-
-
-def pack(atm, ocean, weights, chunks=2):
+
+
+def pack(atm, ocean, chunks=2):
     rows = jax.ShapeDtypeStruct((WIDE + ocean.shape[2], LANES), BF16)
     return pl.pallas_call(
         pack_kernel,
-        in_specs=[HBM, HBM, HBM],
-        out_specs=[VMEM] * 4,
+        in_specs=[HBM, HBM],
+        out_specs=[VMEM] * 3,
         out_shape=[
             rows,
             rows,
             jax.ShapeDtypeStruct((2, 16, WIDE), F32),
-            jax.ShapeDtypeStruct((AHEAD, LANES, LANES), BF16),
         ],
         scratch_shapes=[
             pltpu.VMEM(atm.shape, F32),
             pltpu.VMEM(ocean.shape, F32),
-            pltpu.SemaphoreType.DMA((2,)),
+            pltpu.SemaphoreType.DMA((1,)),
             pltpu.SemaphoreType.DMA((chunks,)),
         ],
         compiler_params=params(24),
-        cost_estimate=cost(1 << 28, 5),
+        cost_estimate=cost(1 << 33, 16),
         name="pack_halo",
-    )(atm, ocean, weights)
+    )(atm, ocean)
 
 
 def fetch_tiles(w_ref, tiles_ref, sems):
@@ -539,12 +535,11 @@
 
 
 def forward_kernel(
-    count_ref, owner_ref, block_ref, source_ref, level_ref, ahead_ref, w_ref, out_ref, place_ref,
-    tiles_ref, picked, contrib, left, sems,
+    count_ref, owner_ref, block_ref, source_ref, level_ref, w_ref, out_ref, place_ref,
+    picked, contrib, left,
 ):
     tiles = owner_ref.shape[1]
     per_row = WIDE // LANES
-    copies = fetch_tiles(w_ref, tiles_ref, sems)
 
     source = source_ref[...]
     cell = (source & (per_row - 1)) * 16 + (source >> (per_row.bit_length() - 1))
@@ -568,7 +563,7 @@
     part = out_ref.shape[0] * GROUP // tiles
 
     for t in range(0, tiles, GROUP):
-        held = held_tiles(t, ahead_ref, tiles_ref, copies)
+        held = w_ref[t : t + GROUP].reshape(GROUP * LANES, LANES)
         row = iota((part, tiles), 0) + t // GROUP * part
         here = slice(t // GROUP * part, (t // GROUP + 1) * part)
         for m, at in enumerate((place, place + CAP, index)):
@@ -587,27 +582,25 @@
     out_ref[...] = out[:, :LANES] + out[:, LANES:]
 
 
-def forward(count, owner, block, source, level, ahead, weights, devices, parts=4):
+def forward(count, owner, block, source, level, weights, devices):
     tiles = weights.shape[0]
     return pl.pallas_call(
         forward_kernel,
-        in_specs=[VMEM] * 6 + [HBM],
+        in_specs=[VMEM] * 6,
         out_specs=[VMEM] * 2,
         out_shape=[
             jax.ShapeDtypeStruct((devices * ROWS, LANES), F32),
             jax.ShapeDtypeStruct((8, tiles), jnp.int32),
         ],
         scratch_shapes=[
-            pltpu.VMEM((tiles - AHEAD, LANES, LANES), BF16),
             pltpu.VMEM((2, tiles, LANES), F32),
             pltpu.VMEM((2, tiles, LANES), F32),
             pltpu.VMEM((devices * ROWS, 3 * tiles), BF16),
-            pltpu.SemaphoreType.DMA((parts,)),
         ],
         compiler_params=params(32),
         cost_estimate=cost(32 * tiles * LANES * LANES, 9),
         name="tiles_forward",
-    )(count, owner, block, source, level, ahead, weights)
+    )(count, owner, block, source, level, weights)
 
 
 def combine_kernel(inbox_ref, ocean_ref, out_ref, flux_ref, boxes):
@@ -753,15 +746,15 @@
 
     atm = pltpu.with_memory_space_constraint(atm, pltpu.HBM)
     sea_state = pltpu.with_memory_space_constraint(ocean, pltpu.HBM)
-    tile_weight = pltpu.with_memory_space_constraint(tile_weight, pltpu.HBM)
+    again = pltpu.with_memory_space_constraint(tile_weight, pltpu.HBM)
     lists = [x.reshape(1, tiles) for x in (tile_owner, tile_block, tile_source)]
-    to_next, to_prev, level, ahead = pack(atm, sea_state, tile_weight)
+    to_next, to_prev, level = pack(atm, sea_state)
     forth = [(i, (i + 1) % devices) for i in range(devices)]
     back = [(target, source) for source, target in forth]
     low = lax.ppermute(to_next, RING, forth)
     high = lax.ppermute(to_prev, RING, back)
     outbox, place = forward(
-        tile_count.reshape(1, 1), *lists, level, ahead, tile_weight, devices
+        tile_count.reshape(1, 1), *lists, level, tile_weight, devices
     )
     inbox = swap(outbox)
     columns = edge_rows(edge, ocean, low, high)
@@ -775,7 +768,7 @@
         edge, atm, ocean, low, high, side, flux, halo, sea, own, half
     )
     returned, whole, ocean_final = lax.optimization_barrier((returned, whole, ocean_final))
-    atm_final = backward(place, returned, tile_weight, zero, one, whole)
+    atm_final = backward(place, returned, again, zero, one, whole)
     return atm_final.reshape(atm_state.shape), ocean_final.reshape(ocean_state.shape)
 
 

time: 62.7 us -> 61.2 us (0.976)
  Pallas kernels: 32.7 us -> 30.3 us
  starting transfers between devices: 22.6 us -> 23.4 us
    pallas_call x2, Pallas kernels: 8.03 us -> 5.71 us  [the longest x1 2.93 us: pack(): pl.pallas_call(pack_kernel, in_specs=[HBM, HBM], out_specs=[VMEM] * 3, ou...]
    ppermute x1, waiting for transfers between devices: 0.01 us -> 0.93 us  [per_device(): high = lax.ppermute(to_prev, RING, back)]
    all_to_all x2, starting transfers between devices: 16.8 us -> 17.7 us  [swap(): lax.all_to_all(boxes, RING, split_axis=0, concat_axis=0, tiled=True)]
    all_to_all x2, waiting for transfers between devices: 5.35 us -> 4.52 us  [swap(): lax.all_to_all(boxes, RING, split_axis=0, concat_axis=0, tiled=True)]
  transfers between devices with their start and end apart: 5 -> 5, of which waited for: 2 -> 3; matrix products, arithmetic and copies ran while one was open for 0% -> 0% of each run, Pallas kernels for 37% -> 34%
where the time goes in v2:
time: 61.2 us; the launch traced here: 61 us
  Pallas kernels  30.3 us (50%)
  starting transfers between devices  23.4 us (38%)
  waiting for transfers between devices  5.46 us (9%)
  between operations  1.62 us (3%)
    all_to_all x2, starting transfers between devices, swap(): lax.all_to_all(boxes, RING, split_axis=0, concat_axis=0, tiled=True)  17.7 us
    pallas_call x1, Pallas kernels, late(): pl.pallas_call(late_kernel, in_specs=[SMEM, HBM] + [VMEM] * 7 + [HBM] * 2...  8.99 us
    pallas_call x1, Pallas kernels, early(): pl.pallas_call(early_kernel, in_specs=[SMEM, VMEM, VMEM, HBM, VMEM, VMEM]...  8.15 us
    pallas_call x1, Pallas kernels, backward(): pl.pallas_call(backward_kernel, in_specs=[VMEM, VMEM, HBM, VMEM, VMEM, HB...  5.6 us
    all_to_all x2, waiting for transfers between devices, swap(): lax.all_to_all(boxes, RING, split_axis=0, concat_axis=0, tiled=True)  4.52 us
    ppermute x1, starting transfers between devices, per_device(): low = lax.ppermute(to_next, RING, forth)  4.37 us
    pallas_call x1, Pallas kernels, pack(): pl.pallas_call(pack_kernel, in_specs=[HBM, HBM], out_specs=[VMEM] * 3, ou...  2.93 us
    pallas_call x1, Pallas kernels, forward(): pl.pallas_call(forward_kernel, in_specs=[VMEM] * 6, out_specs=[VMEM] * 2,...  2.78 us
  transfers between devices with their start and end apart: 5, of which 3 were waited for; matrix products, arithmetic and copies ran while one was open for 0% of the time, Pallas kernels for 34%

profile of v2, /device:TPU:1, one launch (start us, length us, event | category | flops | bytes accessed | tf_op | source)
XLA Modules:
  0.0 61.0 jit_solution(12134059900127664058)
XLA Ops:
  0.6 0.0 slice-start
  0.6 0.0 slice-start.1
  0.7 0.0 copy-start.1
  0.7 0.0 copy-start.2
  0.7 0.0 copy-start.3
  0.7 2.9 %pack_halo.1 = (bf16[2304,128]{1,0:T(8,128)(2,1)S(1)}, bf16[2304,128]{1,0:T(8,128)(2,1)S(1)}, f32[2,16,2048]{2,1,0:T(8,128)S(1)}) custom-call(f32[2,256,2048]{2,1,0:T(8,128)} %bitcast.28, f32[2,128,256]{2,1,0:T(8,128)} %bitcast.20), custom_call_target="tpu_custom_call" | custom-call | flops 8589934592 | bytes 16777216 | tf_op jit(solution)/shard_map/pack_halo/pallas_call | solution.py:495
  3.6 4.4 %collective-permute-start = (bf16[2304,128]{1,0:T(8,128)(2,1)S(1)}, bf16[2304,128]{1,0:T(8,128)(2,1)S(1)}, u32[]{:S(2)}, u32[]{:S(2)}) collective-permute-start(bf16[2304,128]{1,0:T(8,128)(2,1)S(1)} %get-tuple-element.26), channel_id=1, source_target_pairs={{0,1},{1,2},{2,3},{3,4},{4,5},{5,6},{6,7},{7,8},{8,9},{9,10},{10,1... | collective-permute-start | bytes 1769480 | tf_op jit(solution)/shard_map/ppermute | solution.py:754
  8.0 0.0 collective-permute-start.1
  8.6 0.0 slice-done
  8.7 0.0 slice-done.1
  8.7 0.0 copy-done.1
  8.7 0.0 copy-done.2
  8.7 0.0 copy-done.3
  8.7 0.0 copy-start
  8.7 0.0 copy-start.4
  8.7 0.0 copy-start.5
  8.7 2.8 %tiles_forward.1 = (f32[1024,128]{1,0:T(8,128)}, s32[8,256]{1,0:T(8,128)S(1)}) custom-call(s32[1,1]{1,0:T(1,128)} %bitcast.15.count_ref, s32[1,256]{1,0:T(1,128)S(1)} %bitcast.24, s32[1,256]{1,0:T(1,128)S(1)} %bitcast.25, s32[1,256]{1,0:T(1,128)S(1)} %bitcast.26, f32[2,16,2048]{2,1,0:T(8,128)S(1)} %get-tuple-element.23.level_ref, ...), custom_call_target="tpu_custom_call" | custom-call | flops 134217728 | bytes 9437184 | tf_op jit(solution)/shard_map/tiles_forward/pallas_call | solution.py:587
  11.5 10.4 %all-to-all-start = ((f32[128,8,128]{2,1,0:T(8,128)}), f32[128,8,128]{2,1,0:T(8,128)S(1)}, u32[]{:S(2)}, u32[]{:S(2)}) async-start(f32[128,8,128]{2,1,0:T(8,128)} %bitcast.6), calls=%async_computation | async-start | bytes 1048576 | tf_op jit(solution)/shard_map/all_to_all | solution.py:725
  22.0 0.1 pad_add_fusion.edge_ref
  22.1 0.0 collective-permute-done.low_ref
  22.1 0.9 %collective-permute-done.1.high_ref = bf16[2304,128]{1,0:T(8,128)(2,1)S(1)} collective-permute-done((bf16[2304,128]{1,0:T(8,128)(2,1)S(1)}, bf16[2304,128]{1,0:T(8,128)(2,1)S(1)}, u32[]{:S(2)}, u32[]{:S(2)}) %collective-permute-start.1) | collective-permute-done | bytes 589856 | tf_op jit(solution)/shard_map/ppermute | solution.py:755
  23.0 0.0 copy-done
  23.0 0.6 %ocean_edge.1 = f32[32,128]{1,0:T(8,128)S(1)} custom-call(s32[3]{0:T(128)S(1)} %pad_add_fusion.edge_ref, f32[2,128,256]{2,1,0:T(8,128)S(1)} %bitcast.21, bf16[2304,128]{1,0:T(8,128)(2,1)S(1)} %collective-permute-done.low_ref, bf16[2304,128]{1,0:T(8,128)(2,1)S(1)} %collective-permute-done.1.high_ref), custom_call_target="tpu_custom_call" | custom-call | tf_op jit(solution)/shard_map/ocean_edge/pallas_call | solution.py:320
  23.6 1.4 %collective-permute-start.2 = (f32[32,128]{1,0:T(8,128)S(1)}, f32[32,128]{1,0:T(8,128)S(1)}, u32[]{:S(2)}, u32[]{:S(2)}) collective-permute-start(f32[32,128]{1,0:T(8,128)S(1)} %ocean_edge.1), channel_id=1, source_target_pairs={{0,64},{64,0},{1,65},{65,1},{2,66},{66,2},{3,67},{67,3},{4,68},{68... | collective-permute-start | bytes 49160 | tf_op jit(solution)/shard_map/ppermute | solution.py:761
  25.0 0.0 copy-done.4
  25.0 0.0 copy-done.5
  25.0 8.1 %atmosphere_0.1 = (f32[2,256,2048]{2,1,0:T(8,128)}, f32[16,2048]{1,0:T(8,128)S(1)}, bf16[128,1024]{1,0:T(8,128)(2,1)S(1)}, bf16[384,512]{1,0:T(8,128)(2,1)S(1)}, bf16[768,512]{1,0:T(8,128)(2,1)}) custom-call(s32[3]{0:T(128)S(1)} %pad_add_fusion.edge_ref, f32[16,16]{1,0:T(8,128)S(1)} %copy-done.4, f32[16,16]{1,0:T(8,128)S(1)} %copy-done.5, ...), custom_call_target="tpu_custom_call" | custom-call | flops 3221225472 | bytes 6291456 | tf_op jit(solution)/shard_map/atmosphere_0/pallas_call | solution.py:352
  33.2 2.4 %all-to-all-done = f32[128,8,128]{2,1,0:T(8,128)S(1)} async-done(((f32[128,8,128]{2,1,0:T(8,128)}), f32[128,8,128]{2,1,0:T(8,128)S(1)}, u32[]{:S(2)}, u32[]{:S(2)}) %all-to-all-start) | async-done | bytes 524320 | tf_op jit(solution)/shard_map/all_to_all | solution.py:725
  35.6 0.0 collective-permute-done.2.side_ref
  35.6 1.3 %ocean_flux.1 = (bf16[1024,128]{1,0:T(8,128)(2,1)}, f32[2,8,256]{2,1,0:T(8,128)S(1)}) custom-call(f32[1024,128]{1,0:T(8,128)S(1)} %bitcast.18, f32[2,128,256]{2,1,0:T(8,128)S(1)} %bitcast.22), custom_call_target="tpu_custom_call" | custom-call | tf_op jit(solution)/shard_map/ocean_flux/pallas_call | solution.py:645
  36.9 7.2 %all-to-all-start.1 = ((bf16[128,8,128]{2,1,0:T(8,128)(2,1)}), bf16[128,8,128]{2,1,0:T(8,128)(2,1)S(1)}, u32[]{:S(2)}, u32[]{:S(2)}) async-start(bf16[128,8,128]{2,1,0:T(8,128)(2,1)} %bitcast.11), calls=%async_computation.1 | async-start | bytes 524288 | tf_op jit(solution)/shard_map/all_to_all | solution.py:725
  44.1 9.0 %atmosphere_1.1 = (f32[2,256,2048]{2,1,0:T(8,128)}, f32[16,2048]{1,0:T(8,128)S(1)}, f32[2,128,256]{2,1,0:T(8,128)}) custom-call(s32[3]{0:T(128)S(1)} %pad_add_fusion.edge_ref, f32[2,256,2048]{2,1,0:T(8,128)} %bitcast.30, f32[2,128,256]{2,1,0:T(8,128)S(1)} %bitcast.23, ...), custom_call_target="tpu_custom_call", output_to_operand_aliasing={{0}: (10, {})} | custom-call | flops 3221225472 | bytes 6291456 | tf_op jit(solution)/shard_map/atmosphere_1/pallas_call | solution.py:439
  53.1 2.1 %all-to-all-done.1 = bf16[128,8,128]{2,1,0:T(8,128)(2,1)S(1)} async-done(((bf16[128,8,128]{2,1,0:T(8,128)(2,1)}), bf16[128,8,128]{2,1,0:T(8,128)(2,1)S(1)}, u32[]{:S(2)}, u32[]{:S(2)}) %all-to-all-start.1) | async-done | bytes 262176 | tf_op jit(solution)/shard_map/all_to_all | solution.py:725
  55.2 5.6 %tiles_backward.1 = f32[2,256,2048]{2,1,0:T(8,128)} custom-call(s32[8,256]{1,0:T(8,128)S(1)} %get-tuple-element.24.place_ref, bf16[1024,128]{1,0:T(8,128)(2,1)S(1)} %bitcast.19, bf16[256,128,128]{2,1,0:T(8,128)(2,1)} %w_ref.3, f32[16,2048]{1,0:T(8,128)S(1)} %get-tuple-element.40.zero_ref, ...), custom_call_target="tpu_custom_call", output_to_operand_aliasing={{}: (5, {})} | custom-call | flops 134217728 | bytes 1048576 | tf_op jit(solution)/shard_map/tiles_backward/pallas_call | solution.py:702
  (1 shorter events, 0.0 us)
Async XLA Ops:
  0.6 8.0 %slice-start = ((s8[8388608]{0:T(1024)(128)(4,1)}), s8[4194304]{0:T(1024)(128)(4,1)S(1)}, s32[]{:S(2)}) async-start(s8[8388608]{0:T(1024)(128)(4,1)} %bitcast.16), calls=%async_computation.2 | async-start | bytes 8388608
  0.6 8.0 %slice-start.1 = ((s8[8388608]{0:T(1024)(128)(4,1)}), s8[4194304]{0:T(1024)(128)(4,1)S(1)}, s32[]{:S(2)}) async-start(s8[8388608]{0:T(1024)(128)(4,1)} %bitcast.16), calls=%async_computation.3 | async-start | bytes 8388608
  0.7 8.0 %copy-start.1 = (s32[256,1]{0,1:T(1,128)S(1)}, s32[256,1]{0,1:T(1,128)}, u32[]{:S(2)}) copy-start(s32[256,1]{0,1:T(1,128)} %param.14) | copy-start | bytes 3076
  0.7 8.0 %copy-start.2 = (s32[256]{0:T(256)S(1)}, s32[256]{0:T(256)}, u32[]{:S(2)}) copy-start(s32[256]{0:T(256)} %param.15) | copy-start | bytes 3076
  0.7 8.0 %copy-start.3 = (s32[256]{0:T(256)S(1)}, s32[256]{0:T(256)}, u32[]{:S(2)}) copy-start(s32[256]{0:T(256)} %param.16) | copy-start | bytes 3076
  3.6 18.4 %collective-permute-start = (bf16[2304,128]{1,0:T(8,128)(2,1)S(1)}, bf16[2304,128]{1,0:T(8,128)(2,1)S(1)}, u32[]{:S(2)}, u32[]{:S(2)}) collective-permute-start(bf16[2304,128]{1,0:T(8,128)(2,1)S(1)} %get-tuple-element.26), channel_id=1, source_target_pairs={{0,1},{1,2},{2,3},{3,4},{4,5},{5,6},{6,7},{7,8},{8,9},{9,10},{10,1... | collective-permute-start | bytes 1769480 | tf_op jit(solution)/shard_map/ppermute | solution.py:754
  8.0 15.0 %collective-permute-start.1 = (bf16[2304,128]{1,0:T(8,128)(2,1)S(1)}, bf16[2304,128]{1,0:T(8,128)(2,1)S(1)}, u32[]{:S(2)}, u32[]{:S(2)}) collective-permute-start(bf16[2304,128]{1,0:T(8,128)(2,1)S(1)} %get-tuple-element.27), channel_id=1, source_target_pairs={{1,0},{2,1},{3,2},{4,3},{5,4},{6,5},{7,6},{8,7},{9,8},{10,9},{11,1... | collective-permute-start | bytes 1769480 | tf_op jit(solution)/shard_map/ppermute | solution.py:755
  8.7 14.3 %copy-start = (f32[2,16,8,256]{3,2,1,0:T(8,128)S(1)}, f32[2,16,8,256]{3,2,1,0:T(8,128)}, u32[]{:S(2)}) copy-start(f32[2,16,8,256]{3,2,1,0:T(8,128)} %param.10) | copy-start | bytes 786436
  8.7 16.3 %copy-start.4 = (f32[16,16]{1,0:T(8,128)S(1)}, f32[16,16]{1,0:T(8,128)}, u32[]{:S(2)}) copy-start(f32[16,16]{1,0:T(8,128)} %atm_levels_ref.1) | copy-start | bytes 3076
  8.7 16.3 %copy-start.5 = (f32[16,16]{1,0:T(8,128)S(1)}, f32[16,16]{1,0:T(8,128)}, u32[]{:S(2)}) copy-start(f32[16,16]{1,0:T(8,128)} %ocean_levels_ref.1) | copy-start | bytes 3076
  11.5 24.1 %all-to-all-start = ((f32[128,8,128]{2,1,0:T(8,128)}), f32[128,8,128]{2,1,0:T(8,128)S(1)}, u32[]{:S(2)}, u32[]{:S(2)}) async-start(f32[128,8,128]{2,1,0:T(8,128)} %bitcast.6), calls=%async_computation | async-start | bytes 1048576 | tf_op jit(solution)/shard_map/all_to_all | solution.py:725
  23.6 12.0 %collective-permute-start.2 = (f32[32,128]{1,0:T(8,128)S(1)}, f32[32,128]{1,0:T(8,128)S(1)}, u32[]{:S(2)}, u32[]{:S(2)}) collective-permute-start(f32[32,128]{1,0:T(8,128)S(1)} %ocean_edge.1), channel_id=1, source_target_pairs={{0,64},{64,0},{1,65},{65,1},{2,66},{66,2},{3,67},{67,3},{4,68},{68... | collective-permute-start | bytes 49160 | tf_op jit(solution)/shard_map/ppermute | solution.py:761
  36.9 18.3 %all-to-all-start.1 = ((bf16[128,8,128]{2,1,0:T(8,128)(2,1)}), bf16[128,8,128]{2,1,0:T(8,128)(2,1)S(1)}, u32[]{:S(2)}, u32[]{:S(2)}) async-start(bf16[128,8,128]{2,1,0:T(8,128)(2,1)} %bitcast.11), calls=%async_computation.1 | async-start | bytes 524288 | tf_op jit(solution)/shard_map/all_to_all | solution.py:725

commit v3 on v2

--- a/solution.py
+++ b/solution.py
@@ -225,9 +225,9 @@
                 left, main, minor, w, held, sems):
     chunks = len(arrivals)
     size = WIDE // chunks
-    main[0:512] = own_ref[0:512]
-    main[512:768] = own_ref[256:512]
-    main[768:1024] = halo_rows(halo_ref[:, 0:512], v)
+    main[0:256] = own_ref[256:512]
+    main[256:512] = own_ref[256:512]
+    main[512:768] = halo_rows(halo_ref[:, 0:512], v)
     minor[0:256] = own_ref[512:768]
     minor[256:512] = halo_rows(halo_ref[:, 512:1024], v)
     copies = []
@@ -243,16 +243,16 @@
                     high, low = split(state)
                     lanes = slice(h * LANES, (h + 1) * LANES)
                     w[STEPS, PAD + at : PAD + at + LANES, lanes] = state * diffuse**STEPS
-                    left[rows, h * LANES : (h + 1) * LANES] = high
-                    left[rows, 256 + h * LANES : 256 + (h + 1) * LANES] = low
-                    left[rows, 512 + h * LANES : 512 + (h + 1) * LANES] = high
-            left[:, 768:896] = low_ref[start : start + size]
-            left[:, 896:1024] = high_ref[start : start + size]
+                    left[rows, h * LANES : (h + 1) * LANES] = low
+                    left[rows, 256 + h * LANES : 256 + (h + 1) * LANES] = high
+            left[:, 512:640] = low_ref[start : start + size]
+            left[:, 640:768] = high_ref[start : start + size]
             rows = slice(PAD + start, PAD + start + size)
             for s in range(2):
                 lanes = slice(s * 256, (s + 1) * 256)
-                w[s, rows] = mxu(left[...], main[:, lanes])
-                w[2 + s, rows] = mxu(left[:, 512:1024], minor[:, lanes])
+                fine = mxu(left[:, 256:512], own_ref[0:256, lanes])
+                w[s, rows] = mxu(left[...], main[:, lanes]) + fine
+                w[2 + s, rows] = mxu(left[:, 256:768], minor[:, lanes])
         if n == 0:
             for s in range(1, STEPS + 1):
                 w[s, 0:PAD] = mirror_low(w[s, PAD : 2 * PAD])
@@ -285,8 +285,8 @@
     return [
         pltpu.VMEM((256, WIDE), F32),
         pltpu.SemaphoreType.DMA((chunks,)),
-        pltpu.VMEM((size, 1024), BF16),
-        pltpu.VMEM((1024, 512), BF16),
+        pltpu.VMEM((size, 768), BF16),
+        pltpu.VMEM((768, 512), BF16),
         pltpu.VMEM((512, 512), BF16),
         pltpu.VMEM((STEPS + 1, WIDE + 2 * PAD, 256), F32),
         pltpu.VMEM((256, WIDE), F32),

time: 61.2 us -> 61.1 us (level)
  transfers between devices with their start and end apart: 5 -> 5, of which waited for: 3 -> 3; matrix products, arithmetic and copies ran while one was open for 0% -> 0% of each run, Pallas kernels for 34% -> 33%
where the time goes in v3:
time: 61.1 us; the launch traced here: 60.8 us
  Pallas kernels  30 us (49%)
  starting transfers between devices  23.3 us (38%)
  waiting for transfers between devices  5.76 us (9%)
  between operations  1.62 us (3%)
    all_to_all x2, starting transfers between devices, swap(): lax.all_to_all(boxes, RING, split_axis=0, concat_axis=0, tiled=True)  17.5 us
    pallas_call x1, Pallas kernels, late(): pl.pallas_call(late_kernel, in_specs=[SMEM, HBM] + [VMEM] * 7 + [HBM] * 2...  8.83 us
    pallas_call x1, Pallas kernels, early(): pl.pallas_call(early_kernel, in_specs=[SMEM, VMEM, VMEM, HBM, VMEM, VMEM]...  8 us
    pallas_call x1, Pallas kernels, backward(): pl.pallas_call(backward_kernel, in_specs=[VMEM, VMEM, HBM, VMEM, VMEM, HB...  5.6 us
    all_to_all x2, waiting for transfers between devices, swap(): lax.all_to_all(boxes, RING, split_axis=0, concat_axis=0, tiled=True)  4.82 us
    ppermute x1, starting transfers between devices, per_device(): low = lax.ppermute(to_next, RING, forth)  4.37 us
    pallas_call x1, Pallas kernels, pack(): pl.pallas_call(pack_kernel, in_specs=[HBM, HBM], out_specs=[VMEM] * 3, ou...  2.93 us
    pallas_call x1, Pallas kernels, forward(): pl.pallas_call(forward_kernel, in_specs=[VMEM] * 6, out_specs=[VMEM] * 2,...  2.78 us
  transfers between devices with their start and end apart: 5, of which 3 were waited for; matrix products, arithmetic and copies ran while one was open for 0% of the time, Pallas kernels for 33%

profile of v3, /device:TPU:1, one launch (start us, length us, event | category | flops | bytes accessed | tf_op | source)
XLA Modules:
  0.0 60.8 jit_solution(12895202272856255172)
XLA Ops:
  0.6 0.0 slice-start
  0.6 0.0 slice-start.1
  0.7 0.0 copy-start.1
  0.7 0.0 copy-start.2
  0.7 0.0 copy-start.3
  0.7 2.9 %pack_halo.1 = (bf16[2304,128]{1,0:T(8,128)(2,1)S(1)}, bf16[2304,128]{1,0:T(8,128)(2,1)S(1)}, f32[2,16,2048]{2,1,0:T(8,128)S(1)}) custom-call(f32[2,256,2048]{2,1,0:T(8,128)} %bitcast.28, f32[2,128,256]{2,1,0:T(8,128)} %bitcast.20), custom_call_target="tpu_custom_call" | custom-call | flops 8589934592 | bytes 16777216 | tf_op jit(solution)/shard_map/pack_halo/pallas_call | solution.py:495
  3.6 4.4 %collective-permute-start = (bf16[2304,128]{1,0:T(8,128)(2,1)S(1)}, bf16[2304,128]{1,0:T(8,128)(2,1)S(1)}, u32[]{:S(2)}, u32[]{:S(2)}) collective-permute-start(bf16[2304,128]{1,0:T(8,128)(2,1)S(1)} %get-tuple-element.26), channel_id=1, source_target_pairs={{0,1},{1,2},{2,3},{3,4},{4,5},{5,6},{6,7},{7,8},{8,9},{9,10},{10,1... | collective-permute-start | bytes 1769480 | tf_op jit(solution)/shard_map/ppermute | solution.py:754
  8.0 0.0 collective-permute-start.1
  8.6 0.0 slice-done
  8.7 0.0 slice-done.1
  8.7 0.0 copy-done.1
  8.7 0.0 copy-done.2
  8.7 0.0 copy-done.3
  8.7 0.0 copy-start
  8.7 0.0 copy-start.4
  8.7 0.0 copy-start.5
  8.7 2.8 %tiles_forward.1 = (f32[1024,128]{1,0:T(8,128)}, s32[8,256]{1,0:T(8,128)S(1)}) custom-call(s32[1,1]{1,0:T(1,128)} %bitcast.15.count_ref, s32[1,256]{1,0:T(1,128)S(1)} %bitcast.24, s32[1,256]{1,0:T(1,128)S(1)} %bitcast.25, s32[1,256]{1,0:T(1,128)S(1)} %bitcast.26, f32[2,16,2048]{2,1,0:T(8,128)S(1)} %get-tuple-element.23.level_ref, ...), custom_call_target="tpu_custom_call" | custom-call | flops 134217728 | bytes 9437184 | tf_op jit(solution)/shard_map/tiles_forward/pallas_call | solution.py:587
  11.5 10.4 %all-to-all-start = ((f32[128,8,128]{2,1,0:T(8,128)}), f32[128,8,128]{2,1,0:T(8,128)S(1)}, u32[]{:S(2)}, u32[]{:S(2)}) async-start(f32[128,8,128]{2,1,0:T(8,128)} %bitcast.6), calls=%async_computation | async-start | bytes 1048576 | tf_op jit(solution)/shard_map/all_to_all | solution.py:725
  22.0 0.1 pad_add_fusion.edge_ref
  22.1 0.0 collective-permute-done.low_ref
  22.1 0.9 %collective-permute-done.1.high_ref = bf16[2304,128]{1,0:T(8,128)(2,1)S(1)} collective-permute-done((bf16[2304,128]{1,0:T(8,128)(2,1)S(1)}, bf16[2304,128]{1,0:T(8,128)(2,1)S(1)}, u32[]{:S(2)}, u32[]{:S(2)}) %collective-permute-start.1) | collective-permute-done | bytes 589856 | tf_op jit(solution)/shard_map/ppermute | solution.py:755
  23.0 0.0 copy-done
  23.0 0.6 %ocean_edge.1 = f32[32,128]{1,0:T(8,128)S(1)} custom-call(s32[3]{0:T(128)S(1)} %pad_add_fusion.edge_ref, f32[2,128,256]{2,1,0:T(8,128)S(1)} %bitcast.21, bf16[2304,128]{1,0:T(8,128)(2,1)S(1)} %collective-permute-done.low_ref, bf16[2304,128]{1,0:T(8,128)(2,1)S(1)} %collective-permute-done.1.high_ref), custom_call_target="tpu_custom_call" | custom-call | tf_op jit(solution)/shard_map/ocean_edge/pallas_call | solution.py:320
  23.6 1.4 %collective-permute-start.2 = (f32[32,128]{1,0:T(8,128)S(1)}, f32[32,128]{1,0:T(8,128)S(1)}, u32[]{:S(2)}, u32[]{:S(2)}) collective-permute-start(f32[32,128]{1,0:T(8,128)S(1)} %ocean_edge.1), channel_id=1, source_target_pairs={{0,64},{64,0},{1,65},{65,1},{2,66},{66,2},{3,67},{67,3},{4,68},{68... | collective-permute-start | bytes 49160 | tf_op jit(solution)/shard_map/ppermute | solution.py:761
  25.0 0.0 copy-done.4
  25.0 0.0 copy-done.5
  25.0 8.0 %atmosphere_0.1 = (f32[2,256,2048]{2,1,0:T(8,128)}, f32[16,2048]{1,0:T(8,128)S(1)}, bf16[128,1024]{1,0:T(8,128)(2,1)S(1)}, bf16[384,512]{1,0:T(8,128)(2,1)S(1)}, bf16[768,512]{1,0:T(8,128)(2,1)}) custom-call(s32[3]{0:T(128)S(1)} %pad_add_fusion.edge_ref, f32[16,16]{1,0:T(8,128)S(1)} %copy-done.4, f32[16,16]{1,0:T(8,128)S(1)} %copy-done.5, ...), custom_call_target="tpu_custom_call" | custom-call | flops 3221225472 | bytes 6291456 | tf_op jit(solution)/shard_map/atmosphere_0/pallas_call | solution.py:352
  33.0 2.6 %all-to-all-done = f32[128,8,128]{2,1,0:T(8,128)S(1)} async-done(((f32[128,8,128]{2,1,0:T(8,128)}), f32[128,8,128]{2,1,0:T(8,128)S(1)}, u32[]{:S(2)}, u32[]{:S(2)}) %all-to-all-start) | async-done | bytes 524320 | tf_op jit(solution)/shard_map/all_to_all | solution.py:725
  35.6 0.0 collective-permute-done.2.side_ref
  35.6 1.3 %ocean_flux.1 = (bf16[1024,128]{1,0:T(8,128)(2,1)}, f32[2,8,256]{2,1,0:T(8,128)S(1)}) custom-call(f32[1024,128]{1,0:T(8,128)S(1)} %bitcast.18, f32[2,128,256]{2,1,0:T(8,128)S(1)} %bitcast.22), custom_call_target="tpu_custom_call" | custom-call | tf_op jit(solution)/shard_map/ocean_flux/pallas_call | solution.py:645
  36.9 7.1 %all-to-all-start.1 = ((bf16[128,8,128]{2,1,0:T(8,128)(2,1)}), bf16[128,8,128]{2,1,0:T(8,128)(2,1)S(1)}, u32[]{:S(2)}, u32[]{:S(2)}) async-start(bf16[128,8,128]{2,1,0:T(8,128)(2,1)} %bitcast.11), calls=%async_computation.1 | async-start | bytes 524288 | tf_op jit(solution)/shard_map/all_to_all | solution.py:725
  44.0 8.8 %atmosphere_1.1 = (f32[2,256,2048]{2,1,0:T(8,128)}, f32[16,2048]{1,0:T(8,128)S(1)}, f32[2,128,256]{2,1,0:T(8,128)}) custom-call(s32[3]{0:T(128)S(1)} %pad_add_fusion.edge_ref, f32[2,256,2048]{2,1,0:T(8,128)} %bitcast.30, f32[2,128,256]{2,1,0:T(8,128)S(1)} %bitcast.23, ...), custom_call_target="tpu_custom_call", output_to_operand_aliasing={{0}: (10, {})} | custom-call | flops 3221225472 | bytes 6291456 | tf_op jit(solution)/shard_map/atmosphere_1/pallas_call | solution.py:439
  52.8 2.2 %all-to-all-done.1 = bf16[128,8,128]{2,1,0:T(8,128)(2,1)S(1)} async-done(((bf16[128,8,128]{2,1,0:T(8,128)(2,1)}), bf16[128,8,128]{2,1,0:T(8,128)(2,1)S(1)}, u32[]{:S(2)}, u32[]{:S(2)}) %all-to-all-start.1) | async-done | bytes 262176 | tf_op jit(solution)/shard_map/all_to_all | solution.py:725
  55.0 5.6 %tiles_backward.1 = f32[2,256,2048]{2,1,0:T(8,128)} custom-call(s32[8,256]{1,0:T(8,128)S(1)} %get-tuple-element.24.place_ref, bf16[1024,128]{1,0:T(8,128)(2,1)S(1)} %bitcast.19, bf16[256,128,128]{2,1,0:T(8,128)(2,1)} %w_ref.3, f32[16,2048]{1,0:T(8,128)S(1)} %get-tuple-element.40.zero_ref, ...), custom_call_target="tpu_custom_call", output_to_operand_aliasing={{}: (5, {})} | custom-call | flops 134217728 | bytes 1048576 | tf_op jit(solution)/shard_map/tiles_backward/pallas_call | solution.py:702
  (1 shorter events, 0.0 us)
Async XLA Ops:
  0.6 8.0 %slice-start = ((s8[8388608]{0:T(1024)(128)(4,1)}), s8[4194304]{0:T(1024)(128)(4,1)S(1)}, s32[]{:S(2)}) async-start(s8[8388608]{0:T(1024)(128)(4,1)} %bitcast.16), calls=%async_computation.2 | async-start | bytes 8388608
  0.6 8.0 %slice-start.1 = ((s8[8388608]{0:T(1024)(128)(4,1)}), s8[4194304]{0:T(1024)(128)(4,1)S(1)}, s32[]{:S(2)}) async-start(s8[8388608]{0:T(1024)(128)(4,1)} %bitcast.16), calls=%async_computation.3 | async-start | bytes 8388608
  0.7 8.0 %copy-start.1 = (s32[256,1]{0,1:T(1,128)S(1)}, s32[256,1]{0,1:T(1,128)}, u32[]{:S(2)}) copy-start(s32[256,1]{0,1:T(1,128)} %param.14) | copy-start | bytes 3076
  0.7 8.0 %copy-start.2 = (s32[256]{0:T(256)S(1)}, s32[256]{0:T(256)}, u32[]{:S(2)}) copy-start(s32[256]{0:T(256)} %param.15) | copy-start | bytes 3076
  0.7 8.0 %copy-start.3 = (s32[256]{0:T(256)S(1)}, s32[256]{0:T(256)}, u32[]{:S(2)}) copy-start(s32[256]{0:T(256)} %param.16) | copy-start | bytes 3076
  3.6 18.4 %collective-permute-start = (bf16[2304,128]{1,0:T(8,128)(2,1)S(1)}, bf16[2304,128]{1,0:T(8,128)(2,1)S(1)}, u32[]{:S(2)}, u32[]{:S(2)}) collective-permute-start(bf16[2304,128]{1,0:T(8,128)(2,1)S(1)} %get-tuple-element.26), channel_id=1, source_target_pairs={{0,1},{1,2},{2,3},{3,4},{4,5},{5,6},{6,7},{7,8},{8,9},{9,10},{10,1... | collective-permute-start | bytes 1769480 | tf_op jit(solution)/shard_map/ppermute | solution.py:754
  8.0 15.0 %collective-permute-start.1 = (bf16[2304,128]{1,0:T(8,128)(2,1)S(1)}, bf16[2304,128]{1,0:T(8,128)(2,1)S(1)}, u32[]{:S(2)}, u32[]{:S(2)}) collective-permute-start(bf16[2304,128]{1,0:T(8,128)(2,1)S(1)} %get-tuple-element.27), channel_id=1, source_target_pairs={{1,0},{2,1},{3,2},{4,3},{5,4},{6,5},{7,6},{8,7},{9,8},{10,9},{11,1... | collective-permute-start | bytes 1769480 | tf_op jit(solution)/shard_map/ppermute | solution.py:755
  8.7 14.3 %copy-start = (f32[2,16,8,256]{3,2,1,0:T(8,128)S(1)}, f32[2,16,8,256]{3,2,1,0:T(8,128)}, u32[]{:S(2)}) copy-start(f32[2,16,8,256]{3,2,1,0:T(8,128)} %param.10) | copy-start | bytes 786436
  8.7 16.3 %copy-start.4 = (f32[16,16]{1,0:T(8,128)S(1)}, f32[16,16]{1,0:T(8,128)}, u32[]{:S(2)}) copy-start(f32[16,16]{1,0:T(8,128)} %atm_levels_ref.1) | copy-start | bytes 3076
  8.7 16.3 %copy-start.5 = (f32[16,16]{1,0:T(8,128)S(1)}, f32[16,16]{1,0:T(8,128)}, u32[]{:S(2)}) copy-start(f32[16,16]{1,0:T(8,128)} %ocean_levels_ref.1) | copy-start | bytes 3076
  11.5 24.1 %all-to-all-start = ((f32[128,8,128]{2,1,0:T(8,128)}), f32[128,8,128]{2,1,0:T(8,128)S(1)}, u32[]{:S(2)}, u32[]{:S(2)}) async-start(f32[128,8,128]{2,1,0:T(8,128)} %bitcast.6), calls=%async_computation | async-start | bytes 1048576 | tf_op jit(solution)/shard_map/all_to_all | solution.py:725
  23.6 12.0 %collective-permute-start.2 = (f32[32,128]{1,0:T(8,128)S(1)}, f32[32,128]{1,0:T(8,128)S(1)}, u32[]{:S(2)}, u32[]{:S(2)}) collective-permute-start(f32[32,128]{1,0:T(8,128)S(1)} %ocean_edge.1), channel_id=1, source_target_pairs={{0,64},{64,0},{1,65},{65,1},{2,66},{66,2},{3,67},{67,3},{4,68},{68... | collective-permute-start | bytes 49160 | tf_op jit(solution)/shard_map/ppermute | solution.py:761
  36.9 18.2 %all-to-all-start.1 = ((bf16[128,8,128]{2,1,0:T(8,128)(2,1)}), bf16[128,8,128]{2,1,0:T(8,128)(2,1)S(1)}, u32[]{:S(2)}, u32[]{:S(2)}) async-start(bf16[128,8,128]{2,1,0:T(8,128)(2,1)} %bitcast.11), calls=%async_computation.1 | async-start | bytes 524288 | tf_op jit(solution)/shard_map/all_to_all | solution.py:725
